TPU v7x, 256 devices: a whole 4x4x8 slice. The times are simulated.
256 devices in a mesh: rows: 16 (over x, y), cols: 16 (over z, core).
Axes of the slice: x: 4, y: 4, z: 8, core: 2. Of those that a mesh axis runs over, the one named last changes fastest.
Arguments:
- weight: float32 [12288, 16384], P(('rows', 'cols')), may hold values from -6 to 6
- factor_panel: float32 [2, 16, 512, 1024], P(None, 'cols'), may hold values from -0.1875 to 0.1875
- diag_inverse: float32 [2, 512, 512], P(None, 'rows'), may hold values from -2 to 2, as said below
Outputs:
- whitened: float32 [12288, 2, 16, 512], P('rows', None, 'cols')
Inputs may be any that keep to these rules, and one draw needn't show every extreme that they name: `diag_inverse`: each of the two blocks is lower triangular with diagonal entries between 0.5 and 2.
All inputs are finite; a program needn't handle non-finite values.
Results may differ from a plain program's by a relative error of at most 0.00007.
Values sent between devices are 32-bit elements; how exact they have to be, the bound alone decides.
No kernel may reach another device: no remote copies, remote signals or barrier semaphores. Data moves between devices by JAX's collectives and lax.ppermute only.
A program may use at most 64 MiB of HBM per device.

v0:
```python
import jax
import jax.numpy as jnp
from jax import lax
from jax.sharding import PartitionSpec as P


def from_root(block, axis, holder):
    block = jnp.where(lax.axis_index(axis) == holder, block, jnp.zeros_like(block))
    return lax.psum(block, axis)


def times_transpose(left, right):
    return lax.dot_general(left, right, (((1,), (1,)), ((), ())), precision=lax.Precision.HIGHEST)


def panel_update(solved, panel_part):
    return jnp.einsum("rk,hik->rhi", solved, panel_part, precision=lax.Precision.HIGHEST)


def per_device(weight, factor_panel, diag_inverse):
    col_count = lax.axis_size("cols")
    column = lax.axis_index("cols")
    block_size = factor_panel.shape[2]
    cycles = factor_panel.shape[0]
    inverse_full = lax.all_gather(diag_inverse, "rows", axis=1, tiled=True)
    panel_local = factor_panel[:, 0]
    lower_panel = panel_local[:, :, :block_size]
    upper_panel = panel_local[:, :, block_size:]
    grid_view = weight.reshape(weight.shape[0], cycles, col_count, block_size)
    tile_blocks = lax.all_to_all(grid_view, "cols", split_axis=2, concat_axis=0, tiled=True)[
        :, :, 0, :
    ]
    lead_block = tile_blocks[:, 0]
    rest_blocks = tile_blocks[:, 1:]
    solved_first = from_root(times_transpose(lead_block, inverse_full[0]), "cols", 0)
    lead_once = lead_block - times_transpose(solved_first, lower_panel[0])
    rest_once = rest_blocks - panel_update(solved_first, lower_panel[1:])
    solved_second = from_root(times_transpose(lead_once, inverse_full[1]), "cols", 1)
    lead_twice = lead_once - times_transpose(solved_second, upper_panel[0])
    rest_twice = rest_once - panel_update(solved_second, upper_panel[1:])
    lead_final = jnp.where(
        column == 0, solved_first, jnp.where(column == 1, solved_second, lead_twice)
    )
    result = jnp.concatenate([lead_final[:, None], rest_twice], axis=1)
    return result.reshape(result.shape[0], cycles, 1, block_size)


def solution(mesh):
    placed = (P(("rows", "cols"), None), P(None, "cols", None, None), P(None, "rows", None))
    return jax.shard_map(
        per_device,
        mesh=mesh,
        in_specs=placed,
        out_specs=P("rows", None, "cols", None),
        check_vma=False,
    )
```

profile of v0, /device:TPU:1, one launch (start us, length us, event | category | flops | bytes accessed | tf_op | source)
XLA Modules:
  0.0 361.1 jit_solution(14846679816732798297)
XLA Ops:
  6.5 3.7 %copy.11 = f32[6,8,32,512]{3,2,1,0:T(8,128)S(1)} copy(f32[6,8,32,512]{3,1,2,0:T(8,128)} %bitcast.53) | data formatting | bytes 6291456
  10.2 3.5 copy.8
  13.7 10.0 %all-to-all-start = ((f32[48,2,16,512]{3,0,1,2:T(8,128)}), f32[48,2,16,512]{3,0,1,2:T(8,128)S(1)}, u32[]{:S(2)}, u32[]{:S(2)}) async-start(f32[48,2,16,512]{3,0,1,2:T(8,128)} %copy.8), calls=%async_computation | async-start | bytes 6291456 | tf_op jit(solution)/shard_map/all_to_all | solution.py:30
  23.7 0.0 all-gather.2.cloned.1.call-start
  23.7 0.7 all-gather.2.cloned.1.call-update
  24.4 0.0 all-reduce.3.cloned.1.call-start
  24.5 70.2 %all-to-all-done = f32[48,2,16,512]{3,0,1,2:T(8,128)S(1)} async-done(((f32[48,2,16,512]{3,0,1,2:T(8,128)}), f32[48,2,16,512]{3,0,1,2:T(8,128)S(1)}, u32[]{:S(2)}, u32[]{:S(2)}) %all-to-all-start) | async-done | bytes 3145760 | tf_op jit(solution)/shard_map/all_to_all | solution.py:30
  94.7 0.0 copy-start.1
  94.7 1.7 copy-done.1
  96.3 2.3 copy.9
  98.6 0.0 all-gather.2.cloned.1.call-done
  98.7 5.0 %convolution_select_fusion.1 = f32[768,512]{1,0:T(8,128)} fusion(f32[768,2,512]{2,0,1:T(8,128)S(1)} %bitcast.44, f32[2,512,512]{2,1,0:T(8,128)} %all-gather.2.cloned.1.call-done, pred[]{:T(512)S(6)} %eq.8), kind=kOutput, calls=%fused_computation.6 | convolution fusion | flops 2416312320 | bytes 4194305 | tf_op jit(solution)/shard_map/dot_general | solution.py:13
  103.7 0.0 all-reduce.3.cloned.1.call-update
  103.7 0.2 all-reduce.5.cloned.1.call-start
  103.9 112.2 %all-reduce.3.cloned.1.call-done = f32[768,512]{1,0:T(8,128)} async-done(((f32[768,512]{1,0:T(8,128)}), f32[768,512]{1,0:T(8,128)}) %all-reduce.3.cloned.1.call-update) | async-done | bytes 1572880 | tf_op jit(solution)/shard_map/psum | solution.py:9
  216.2 0.0 copy-start.4
  216.2 4.6 %convolution_subtract_fusion = f32[768,512]{1,0:T(8,128)S(1)} fusion(f32[768,512]{1,0:T(8,128)} %all-reduce.3.cloned.1.call-done, f32[768,2,512]{2,0,1:T(8,128)S(1)} %bitcast.45, f32[2,512,1024]{2,1,0:T(8,128)} %bitcast.49), kind=kOutput, calls=%fused_computation.7 | convolution fusion | flops 2416312320 | bytes 5767168 | tf_op jit(solution)/shard_map/dot_general | solution.py:13
  220.7 0.0 copy-start
  220.7 1.1 copy-done
  221.9 0.0 copy-done.4
  221.9 3.8 %convolution_select_fusion = f32[768,512]{1,0:T(8,128)} fusion(f32[768,512]{1,0:T(8,128)S(1)} %convolution_subtract_fusion, f32[2,512,512]{2,1,0:T(8,128)S(1)} %copy-done.4, pred[]{:T(512)S(6)} %eq.9), kind=kOutput, calls=%fused_computation.5 | convolution fusion | flops 2416312320 | bytes 4194305 | tf_op jit(solution)/shard_map/dot_general | solution.py:13
  225.7 0.0 all-reduce.5.cloned.1.call-update
  225.7 5.5 %fusion.1 = f32[768,512]{1,0:T(8,128)} fusion(f32[768,512]{1,0:T(8,128)} %all-reduce.3.cloned.1.call-done, f32[2,512,1024]{2,1,0:T(8,128)} %bitcast.50), kind=kOutput, calls=%fused_computation.10 | convolution fusion | flops 2415919104 | bytes 4194304 | tf_op jit(solution)/shard_map/rk,hik->rhi/dot_general | solution.py:17
  231.2 108.3 %all-reduce.5.cloned.1.call-done = f32[768,512]{1,0:T(8,128)} async-done(((f32[768,512]{1,0:T(8,128)}), f32[768,512]{1,0:T(8,128)}) %all-reduce.5.cloned.1.call-update) | async-done | bytes 1572880 | tf_op jit(solution)/shard_map/psum | solution.py:9
  339.5 0.0 copy-start.2
  339.5 0.0 copy-start.3
  339.5 5.6 %select_bitcast_fusion = f32[768,1,512]{2,0,1:T(8,128)S(1)} fusion(f32[768,512]{1,0:T(8,128)} %all-reduce.3.cloned.1.call-done, f32[768,512]{1,0:T(8,128)} %all-reduce.5.cloned.1.call-done, f32[768,512]{1,0:T(8,128)} %copy-done, f32[2,512,1024]{2,1,0:T(8,128)} %bitcast.51, pred[]{:T(512)S(6)} %eq.9, pred[]{:T(512)S(6)} %eq.8), kind=kOutput, calls=%fused_computation.4 | convolution fusion | flops 2417098752 | bytes 8912898 | tf_op jit(solution)/shard_map/dot_general | solution.py:13
  345.1 0.0 copy-done.2
  345.1 0.0 copy-done.3
  345.1 4.2 %fusion = f32[768,1,512]{2,0,1:T(8,128)S(1)} fusion(f32[768,2,512]{2,0,1:T(8,128)S(1)} %bitcast.46, f32[768,512]{1,0:T(8,128)S(1)} %copy-done.2, f32[768,512]{1,0:T(8,128)S(1)} %copy-done.3, f32[2,512,1024]{2,1,0:T(8,128)} %bitcast.52), kind=kOutput, calls=%fused_computation.2 | convolution fusion | flops 2416705536 | bytes 7340032 | tf_op jit(solution)/shard_map/rk,hik->rhi/dot_general | solution.py:17
  349.4 0.3 maximum_bitcast_fusion
  349.7 4.9 %copy.10 = f32[768,2,1,512]{3,2,1,0:T(1,128)} copy(f32[768,2,1,512]{3,0,1,2:T(8,128)S(1)} %maximum_bitcast_fusion) | data formatting | bytes 6291456 | tf_op jit(solution)/shard_map/reshape | solution.py:45
Async XLA Ops:
  13.7 81.0 %all-to-all-start = ((f32[48,2,16,512]{3,0,1,2:T(8,128)}), f32[48,2,16,512]{3,0,1,2:T(8,128)S(1)}, u32[]{:S(2)}, u32[]{:S(2)}) async-start(f32[48,2,16,512]{3,0,1,2:T(8,128)} %copy.8), calls=%async_computation | async-start | bytes 6291456 | tf_op jit(solution)/shard_map/all_to_all | solution.py:30
  23.7 75.0 %all-gather.2.cloned.1.call-start = ((), (), s32[]{:S(2)}) async-start(), calls=%async_computation.1 | async-start | bytes 2228224 | tf_op jit(solution)/shard_map/all_gather | solution.py:25
  24.4 191.7 %all-reduce.3.cloned.1.call-start = ((), (), s32[]{:S(2)}) async-start(), calls=%async_computation.2 | async-start | bytes 3145728 | tf_op jit(solution)/shard_map/psum | solution.py:9
  94.7 1.7 copy-start.1
  103.7 235.8 %all-reduce.5.cloned.1.call-start = ((), (), s32[]{:S(2)}) async-start(), calls=%async_computation.3 | async-start | bytes 3145728 | tf_op jit(solution)/shard_map/psum | solution.py:9
  216.2 5.7 %copy-start.4 = (f32[2,512,512]{2,1,0:T(8,128)S(1)}, f32[2,512,512]{2,1,0:T(8,128)}, u32[]{:S(2)}) copy-start(f32[2,512,512]{2,1,0:T(8,128)} %all-gather.2.cloned.1.call-done) | copy-start | bytes 6291460
  220.7 1.2 copy-start
  339.5 5.6 %copy-start.2 = (f32[768,512]{1,0:T(8,128)S(1)}, f32[768,512]{1,0:T(8,128)}, u32[]{:S(2)}) copy-start(f32[768,512]{1,0:T(8,128)} %fusion.1) | copy-start | bytes 4718596
  339.5 5.6 %copy-start.3 = (f32[768,512]{1,0:T(8,128)S(1)}, f32[768,512]{1,0:T(8,128)}, u32[]{:S(2)}) copy-start(f32[768,512]{1,0:T(8,128)} %all-reduce.5.cloned.1.call-done) | copy-start | bytes 4718596
Sparse Core Ops, SparseCore 0:
  27.0 50.1 all-gather.1
  103.8 112.2 all-reduce.2
  225.9 113.6 all-reduce.4
where the time goes:
time: 361 us
  waiting for transfers between devices  291 us (81%)
  matrix products  28.7 us (8%)
  local copies, waits for them, and re-layouts  17.2 us (5%)
  between operations  13.2 us (4%)
  starting transfers between devices  10.3 us (3%)
    psum x2, waiting for transfers between devices, from_root(): return lax.psum(block, axis)  220 us
    all_to_all x1, waiting for transfers between devices, per_device(): lax.all_to_all(grid_view, 'cols', split_axis=2, concat_axis=0, tiled=True)  70.2 us
    dot_general x4, matrix products, times_transpose(): lax.dot_general(left, right, (((1,), (1,)), ((), ())), precision=lax.Prec...  19 us
    all_to_all x1, starting transfers between devices, per_device(): lax.all_to_all(grid_view, 'cols', split_axis=2, concat_axis=0, tiled=True)  9.98 us
    dot_general x2, matrix products, panel_update(): jnp.einsum('rk,hik->rhi', solved, panel_part, precision=lax.Precision.HIG...  9.74 us
  transfers between devices with their start and end apart: 4, of which 3 were waited for; matrix products, arithmetic and copies ran while one was open for 2% of the time, Pallas kernels for 0%

commit v1 on v0

v1 whole, which is shorter than its diff:
```python
import functools

import jax
import jax.numpy as jnp
from jax import lax
from jax.experimental import pallas as pl
from jax.experimental.pallas import tpu as pltpu
from jax.sharding import PartitionSpec as P

B = 512
CHUNKS = ((0, 8), (8, 8), (16, 8), (24, 24))
NT = (((1,), (1,)), ((), ()))
VMEM = pltpu.CompilerParams(vmem_limit_bytes=40 << 20)
SIDE = 4


def dot_exact(left, right):
    return lax.dot_general(left, right, NT, precision=lax.Precision.HIGHEST, preferred_element_type=jnp.float32)


def dot_half(left, right):
    return lax.dot_general(left, right, NT, preferred_element_type=jnp.float32)


def split(value):
    high = value.astype(jnp.bfloat16)
    return high, (value - high.astype(jnp.float32)).astype(jnp.bfloat16)


def pack_body(rows, w_ref, o_ref):
    for c in range(16):
        for h in range(2):
            for k in range(4):
                o_ref[c, h * 4 + k] = w_ref[:, pl.ds((h * 16 + c) * B + k * 128, 128)]


def pack(weight, first, rows):
    return pl.pallas_call(
        functools.partial(pack_body, rows),
        grid=(1,),
        out_shape=jax.ShapeDtypeStruct((16, 8, rows, 128), jnp.float32),
        in_specs=[pl.BlockSpec((rows, weight.shape[1]), lambda i: (first // rows, 0))],
        out_specs=pl.BlockSpec((16, 8, rows, 128), lambda i: (0, 0, 0, 0)),
        compiler_params=VMEM,
        cost_estimate=pl.CostEstimate(flops=0, bytes_accessed=2 * rows * 65536, transcendentals=0),
    )(weight)


def solve_body(own_ref, other_ref, *refs):
    blocks, (x_ref, w_scr, d0_scr, d1_scr, l_scr) = refs[:9], refs[9:]
    r, c = lax.axis_index("rows"), lax.axis_index("cols")
    x, y, z, parity = r // 4, r % 4, c // 2, c % 2
    for q in range(16):
        dx, dy = (q // 4 - x + 4) % 4, (q % 4 - y + 4) % 4
        at_even, at_odd = dx * 4 + dy, dy * 4 + dx
        own = own_ref[jnp.where(parity == 0, at_even, at_odd)]
        other = other_ref[jnp.where(parity == 0, at_odd, at_even)]
        even = jnp.where(parity == 0, own, other)
        odd = jnp.where(parity == 0, other, own)
        d0_scr[32 * q : 32 * q + 32] = even[:32]
        l_scr[32 * q : 32 * q + 32] = odd[:32]
        d1_scr[32 * q : 32 * q + 16] = even[32:]
        d1_scr[32 * q + 16 : 32 * q + 32] = odd[32:]
    for i in range(7):
        w_scr[48 * i : 48 * i + 48] = blocks[i][...]
    w_scr[336:360] = blocks[7][...]
    w_scr[360:384] = blocks[8][...]
    first = dot_exact(w_scr[:, :B], d0_scr[...])
    second = dot_exact(w_scr[:, B:] - dot_exact(first, l_scr[...]), d1_scr[...])
    for i, shift in enumerate((0, 7, 1, 6, 2, 5, 3, 4)):
        at = (z + shift) % 8
        x_ref[at, :, :B] = first[48 * i : 48 * i + 48]
        x_ref[at, :, B:] = second[48 * i : 48 * i + 48]


def solve(own, other, blocks):
    return pl.pallas_call(
        solve_body,
        out_shape=jax.ShapeDtypeStruct((8, 48, 2 * B), jnp.float32),
        scratch_shapes=[
            pltpu.VMEM((384, 2 * B), jnp.float32),
            pltpu.VMEM((B, B), jnp.float32),
            pltpu.VMEM((B, B), jnp.float32),
            pltpu.VMEM((B, B), jnp.float32),
        ],
        compiler_params=VMEM,
        cost_estimate=pl.CostEstimate(flops=6 * 6 * 384 * B * B, bytes_accessed=6 << 20, transcendentals=0),
    )(own, other, *blocks)


def product_body(own_ref, other_ref, panel_ref, p_ref, xh_scr, xl_scr):
    c = lax.axis_index("cols")
    parity = c % 2
    for part, ref in ((parity, own_ref), (1 - parity, other_ref)):
        for z in range(8):
            value = ref[z]
            high, low = split(value)
            at = pl.multiple_of((2 * z + part) * 48, 16)
            xh_scr[pl.ds(at, 48)] = high
            xl_scr[pl.ds(at, 48)] = low

    def step(j, carry):
        h, i = j // 2, j % 2
        lh, ll = split(panel_ref[h, 0, pl.ds(pl.multiple_of(i * 256, 256), 256), :])
        out = dot_half(xh_scr[...], lh) + (dot_half(xl_scr[...], lh) + dot_half(xh_scr[...], ll))
        p_ref[:, :, pl.ds(pl.multiple_of(j * 256, 256), 256)] = out.reshape(16, 48, 256)
        return carry

    lax.fori_loop(0, 4, step, 0)

    for which in range(2):

        @pl.when(c == which)
        def _():
            for part, ref in ((parity, own_ref), (1 - parity, other_ref)):
                for z in range(8):
                    p_ref[2 * z + part, :, :B] = -ref[z, :, which * B : which * B + B]


def product(own, other, panel):
    return pl.pallas_call(
        product_body,
        out_shape=jax.ShapeDtypeStruct((16, 48, 2 * B), jnp.float32),
        scratch_shapes=[pltpu.VMEM((768, 2 * B), jnp.bfloat16), pltpu.VMEM((768, 2 * B), jnp.bfloat16)],
        compiler_params=VMEM,
        cost_estimate=pl.CostEstimate(flops=2 * 3 * 768 * 1024 * 1024, bytes_accessed=10 << 20, transcendentals=0),
    )(own, other, panel)


def finish_body(rows, w_ref, p_ref, *rest):
    o_ref = rest[-1]
    solved = lax.axis_index("cols") < 2
    for s in range(16):
        for k in range(8):
            w = w_ref[s, k]
            if k < 4:
                w = jnp.where(solved, jnp.zeros_like(w), w)
            o_ref[s, pl.ds(k, rows, stride=8), :] = w - p_ref[s, :, k * 128 : k * 128 + 128]


def finish(part, prod, out, first, rows):
    at = first // rows
    extra = [] if out is None else [out]
    return pl.pallas_call(
        functools.partial(finish_body, rows),
        grid=(1,),
        out_shape=jax.ShapeDtypeStruct((16, 384, 128), jnp.float32),
        in_specs=[
            pl.BlockSpec((16, 8, rows, 128), lambda i: (0, 0, 0, 0)),
            pl.BlockSpec((16, rows, 2 * B), lambda i: (0, at, 0)),
        ]
        + [pl.BlockSpec(memory_space=pl.ANY)] * len(extra),
        out_specs=pl.BlockSpec((16, rows * 8, 128), lambda i: (0, at, 0)),
        input_output_aliases={} if out is None else {2: 0},
        compiler_params=VMEM,
        cost_estimate=pl.CostEstimate(flops=rows * 16384, bytes_accessed=3 * rows * 65536, transcendentals=0),
    )(part, prod, *extra)


def plane_shift(amount, first_phase):
    pairs = []
    for x in range(SIDE):
        for y in range(SIDE):
            for c in range(16):
                along_y = first_phase == (c % 2 == 0)
                tx, ty = (x, (y + amount) % SIDE) if along_y else ((x + amount) % SIDE, y)
                pairs.append(((x * SIDE + y) * 16 + c, (tx * SIDE + ty) * 16 + c))
    return pairs


UP = [(i, (i + 2) % 16) for i in range(16)]
DOWN = [(i, (i - 2) % 16) for i in range(16)]
TWIN = [(i, i ^ 1) for i in range(16)]


def along(value, pairs):
    return lax.ppermute(value, "cols", pairs)


def plane_gather(value):
    for phase in (True, False):
        got = [lax.ppermute(value, ("rows", "cols"), plane_shift(a, phase)) for a in (-1, 2, 1)]
        value = jnp.stack([value] + got)
    return value.reshape((16,) + value.shape[2:])


def exchange(part):
    return lax.all_to_all(part, "cols", split_axis=0, concat_axis=0, tiled=True)


def per_device(weight, factor_panel, diag_inverse):
    r, c = lax.axis_index("rows"), lax.axis_index("cols")
    even = c % 2 == 0

    lead = weight[:, : 2 * B]
    slab = lax.dynamic_slice(factor_panel, (0, 0, r * 32, 0), (1, 1, 32, B))[0, 0]
    far = along(slab, [(1, 5)]) + along(slab, [(1, 13)])
    slab = jnp.where(c == 1, slab, far)
    near = along(slab, [(1, 3), (5, 7), (13, 11)]) + along(slab, [(1, 15), (5, 9)])
    slab = jnp.where((c == 1) | (c == 5) | (c == 13), slab, near)

    half = jnp.concatenate(
        [
            jnp.where(even, diag_inverse[0], slab),
            jnp.where(even, diag_inverse[1, :16], diag_inverse[1, 16:]),
        ]
    )
    own = plane_gather(half)
    other = along(own, TWIN)

    blocks = [lead]
    up, down = lead, lead
    parts = []
    for step, (first, rows) in enumerate(CHUNKS):
        if step == 3:
            up, down = up[:24], down[24:]
        up, down = along(up, UP), along(down, DOWN)
        weight, up, down = lax.optimization_barrier((weight, up, down))
        blocks += [up, down]
        parts.append(exchange(pack(weight, first, rows)))

    mine = solve(own, other, blocks)
    theirs = along(mine, TWIN)
    prod = product(mine, theirs, factor_panel)
    out = None
    for part, (first, rows) in zip(parts, CHUNKS):
        out = finish(part, prod, out, first, rows)
    return out.reshape(768, 2, 1, B)


def solution(mesh):
    placed = (P(("rows", "cols"), None), P(None, "cols", None, None), P(None, "rows", None))
    return jax.shard_map(
        per_device,
        mesh=mesh,
        in_specs=placed,
        out_specs=P("rows", None, "cols", None),
        check_vma=False,
    )
```

time: 361 us -> 155 us (0.43)
  waiting for transfers between devices: 291 us -> 52.8 us
  starting transfers between devices: 10.3 us -> 61.1 us
  matrix products: 28.7 us -> 0 us
  Pallas kernels: 0 us -> 21.2 us
  between operations: 13.2 us -> 0.17 us
  other arithmetic: 0.31 us -> 5.26 us
  local copies, waits for them, and re-layouts: 17.2 us -> 13.2 us
    psum x2 -> x0, waiting for transfers between devices: 220 us -> none  [from_root(): return lax.psum(block, axis)]
    all_to_all x1 -> x4, waiting for transfers between devices: 70.2 us -> 13.7 us  [exchange(): return lax.all_to_all(part, 'cols', split_axis=0, concat_axis=0, tiled=True)]
    ppermute x0 -> x20, waiting for transfers between devices: none -> 39.1 us  [the longest x14 27.3 us: along(): return lax.ppermute(value, 'cols', pairs)]
    ppermute x0 -> x20, starting transfers between devices: none -> 36.2 us  [the longest x14 28 us: along(): return lax.ppermute(value, 'cols', pairs)]
    dot_general x6 -> x0, matrix products: 28.7 us -> none  [the longest x4 19 us: times_transpose(): lax.dot_general(left, right, (((1,), (1,)), ((), ())), precision=lax.Prec...]
    pallas_call x0 -> x10, Pallas kernels: none -> 21.2 us  [the longest x4 8.62 us: finish(): pl.pallas_call(functools.partial(finish_body, rows), grid=(1,), out_shape...]
    all_to_all x1 -> x4, starting transfers between devices: 9.98 us -> 25 us  [exchange(): return lax.all_to_all(part, 'cols', split_axis=0, concat_axis=0, tiled=True)]
    reshape x2 -> x0, local copies, waits for them, and re-layouts: 8.39 us -> none  [the longest x1 4.9 us: per_device(): return result.reshape(result.shape[0], cycles, 1, block_size)]
  transfers between devices with their start and end apart: 4 -> 24, of which waited for: 3 -> 14; matrix products, arithmetic and copies ran while one was open for 2% -> 5% of each run, Pallas kernels for 0% -> 12%
where the time goes in v1:
time: 155 us; the launch traced here: 154 us
  starting transfers between devices  61.1 us (39%)
  waiting for transfers between devices  52.8 us (34%)
  Pallas kernels  21.2 us (14%)
  local copies, waits for them, and re-layouts  13.2 us (9%)
  other arithmetic  5.26 us (3%)
    ppermute x14, starting transfers between devices, along(): return lax.ppermute(value, 'cols', pairs)  28 us
    ppermute x14, waiting for transfers between devices, along(): return lax.ppermute(value, 'cols', pairs)  27.3 us
    all_to_all x4, starting transfers between devices, exchange(): return lax.all_to_all(part, 'cols', split_axis=0, concat_axis=0, tiled=True)  25 us
    all_to_all x4, waiting for transfers between devices, exchange(): return lax.all_to_all(part, 'cols', split_axis=0, concat_axis=0, tiled=True)  13.7 us
    ppermute x6, waiting for transfers between devices, plane_gather(): lax.ppermute(value, ('rows', 'cols'), plane_shift(a, phase))  11.8 us
    unnamed x30, local copies, waits for them, and re-layouts  9.89 us
    pallas_call x4, Pallas kernels, finish(): pl.pallas_call(functools.partial(finish_body, rows), grid=(1,), out_shape...  8.62 us
    ppermute x6, starting transfers between devices, plane_gather(): lax.ppermute(value, ('rows', 'cols'), plane_shift(a, phase))  8.14 us
  transfers between devices with their start and end apart: 24, of which 14 were waited for; matrix products, arithmetic and copies ran while one was open for 5% of the time, Pallas kernels for 12%

profile of v1, /device:TPU:1, one launch (start us, length us, event | category | flops | bytes accessed | tf_op | source)
XLA Modules:
  0.0 153.8 jit_solution(4353969106163399420)
XLA Ops:
  0.0 0.9 slice.18.refs_0_
  0.9 2.5 %collective-permute-start = (f32[48,1024]{1,0:T(8,128)S(1)}, f32[48,1024]{1,0:T(8,128)S(1)}, u32[]{:S(2)}, u32[]{:S(2)}) collective-permute-start(f32[48,1024]{1,0:T(8,128)S(1)} %slice.18.refs_0_), channel_id=1, source_target_pairs={{0,2},{1,3},{2,4},{3,5},{4,6},{5,7},{6,8},{7,9},{8,10},{9,11},{10,... | collective-permute-start | bytes 589832 | tf_op jit(solution)/shard_map/ppermute | solution.py:177
  3.5 4.0 %collective-permute-start.1 = (f32[48,1024]{1,0:T(8,128)S(1)}, f32[48,1024]{1,0:T(8,128)}, u32[]{:S(2)}, u32[]{:S(2)}) collective-permute-start(f32[48,1024]{1,0:T(8,128)S(1)} %slice.18.refs_0_), channel_id=1, source_target_pairs={{0,14},{1,15},{2,0},{3,1},{4,2},{5,3},{6,4},{7,5},{8,6},{9,7},{10,... | collective-permute-start | bytes 589832 | tf_op jit(solution)/shard_map/ppermute | solution.py:177
  7.5 4.5 %collective-permute-done.refs_1_ = f32[48,1024]{1,0:T(8,128)S(1)} collective-permute-done((f32[48,1024]{1,0:T(8,128)S(1)}, f32[48,1024]{1,0:T(8,128)S(1)}, u32[]{:S(2)}, u32[]{:S(2)}) %collective-permute-start) | collective-permute-done | bytes 196640 | tf_op jit(solution)/shard_map/ppermute | solution.py:177
  12.1 2.0 %copy-done = f32[48,16384]{1,0:T(8,128)S(1)} copy-done((f32[48,16384]{1,0:T(8,128)S(1)}, f32[48,16384]{1,0:T(8,128)}, u32[]{:S(2)}) %copy-start) | copy-done | bytes 3145752
  14.9 7.2 %all-to-all-start.3 = ((f32[16,8,8,128]{3,2,1,0:T(8,128)}), f32[16,8,8,128]{3,2,1,0:T(8,128)}, u32[]{:S(2)}, u32[]{:S(2)}) async-start(f32[16,8,8,128]{3,2,1,0:T(8,128)} %copy-done.3), calls=%async_computation.3 | async-start | bytes 1048576 | tf_op jit(solution)/shard_map/all_to_all | solution.py:188
  22.1 1.5 dynamic-slice_bitcast_fusion
  23.6 4.8 %collective-permute-start.8 = (f32[32,512]{1,0:T(8,128)}, f32[32,512]{1,0:T(8,128)}, u32[]{:S(2)}, u32[]{:S(2)}) collective-permute-start(f32[32,512]{1,0:T(8,128)} %dynamic-slice_bitcast_fusion), channel_id=1, source_target_pairs={{1,5},{17,21},{33,37},{49,53},{65,69},{81,85},{97,101},{113,117},{... | collective-permute-start | bytes 196616 | tf_op jit(solution)/shard_map/ppermute | solution.py:177
  28.4 2.5 %collective-permute-start.9 = (f32[32,512]{1,0:T(8,128)}, f32[32,512]{1,0:T(8,128)}, u32[]{:S(2)}, u32[]{:S(2)}) collective-permute-start(f32[32,512]{1,0:T(8,128)} %dynamic-slice_bitcast_fusion), channel_id=1, source_target_pairs={{1,13},{17,29},{33,45},{49,61},{65,77},{81,93},{97,109},{113,125},... | collective-permute-start | bytes 196616 | tf_op jit(solution)/shard_map/ppermute | solution.py:177
  30.9 3.0 %collective-permute-done.8 = f32[32,512]{1,0:T(8,128)} collective-permute-done((f32[32,512]{1,0:T(8,128)}, f32[32,512]{1,0:T(8,128)}, u32[]{:S(2)}, u32[]{:S(2)}) %collective-permute-start.8) | collective-permute-done | bytes 65568 | tf_op jit(solution)/shard_map/ppermute | solution.py:177
  34.7 1.5 %add_select_fusion = f32[32,512]{1,0:T(8,128)} fusion(f32[32,512]{1,0:T(8,128)} %collective-permute-done.8, f32[32,512]{1,0:T(8,128)} %collective-permute-done.9, pred[]{:T(512)S(6)} %eq.16, f32[2,1,512,1024]{3,2,1,0:T(8,128)} %panel_ref.1, s32[]{:T(128)S(6)} %select_n.45), kind=kLoop, calls=%fused_computation.4 | loop fusion | flops 32768 | bytes 262149 | tf_op jit(solution)/shard_map/jit(_where)/select_n | solution.py:198
  36.3 1.9 %collective-permute-start.10 = (f32[32,512]{1,0:T(8,128)}, f32[32,512]{1,0:T(8,128)}, u32[]{:S(2)}, u32[]{:S(2)}) collective-permute-start(f32[32,512]{1,0:T(8,128)} %add_select_fusion), channel_id=1, source_target_pairs={{1,3},{5,7},{13,11},{17,19},{21,23},{29,27},{33,35},{37,39},{45,43... | collective-permute-start | bytes 196616 | tf_op jit(solution)/shard_map/ppermute | solution.py:177
  38.2 1.9 %collective-permute-start.11 = (f32[32,512]{1,0:T(8,128)}, f32[32,512]{1,0:T(8,128)}, u32[]{:S(2)}, u32[]{:S(2)}) collective-permute-start(f32[32,512]{1,0:T(8,128)} %add_select_fusion), channel_id=1, source_target_pairs={{1,15},{5,9},{17,31},{21,25},{33,47},{37,41},{49,63},{53,57},{65,7... | collective-permute-start | bytes 196616 | tf_op jit(solution)/shard_map/ppermute | solution.py:177
  40.1 2.7 %collective-permute-start.3 = (f32[48,1024]{1,0:T(8,128)}, f32[48,1024]{1,0:T(8,128)}, u32[]{:S(2)}, u32[]{:S(2)}) collective-permute-start(f32[48,1024]{1,0:T(8,128)} %collective-permute-done.1.refs_2_), channel_id=1, source_target_pairs={{0,14},{1,15},{2,0},{3,1},{4,2},{5,3},{6,4},{7,5},{8,6},{9,7},{10,... | collective-permute-start | bytes 589832 | tf_op jit(solution)/shard_map/ppermute | solution.py:177
  42.8 1.4 select_bitcast_fusion
  44.2 1.8 %collective-permute-done.2.refs_3_ = f32[48,1024]{1,0:T(8,128)} collective-permute-done((f32[48,1024]{1,0:T(8,128)S(1)}, f32[48,1024]{1,0:T(8,128)}, u32[]{:S(2)}, u32[]{:S(2)}) %collective-permute-start.2) | collective-permute-done | bytes 196640 | tf_op jit(solution)/shard_map/ppermute | solution.py:177
  47.5 5.0 %all-to-all-start.2 = ((f32[16,8,8,128]{3,2,1,0:T(8,128)}), f32[16,8,8,128]{3,2,1,0:T(8,128)}, u32[]{:S(2)}, u32[]{:S(2)}) async-start(f32[16,8,8,128]{3,2,1,0:T(8,128)} %copy-done.4), calls=%async_computation.2 | async-start | bytes 1048576 | tf_op jit(solution)/shard_map/all_to_all | solution.py:188
  52.5 0.9 bitcast_select_fusion
  53.5 2.6 %collective-permute-start.12 = (f32[48,512]{1,0:T(8,128)S(1)}, f32[48,512]{1,0:T(8,128)S(1)}, u32[]{:S(2)}, u32[]{:S(2)}) collective-permute-start(f32[48,512]{1,0:T(8,128)S(1)} %get-tuple-element.32), channel_id=1, source_target_pairs={{0,48},{1,193},{2,50},{3,195},{4,52},{5,197},{6,54},{7,199},{8,56}... | collective-permute-start | bytes 294920 | tf_op jit(solution)/shard_map/ppermute | solution.py:182
  57.7 3.7 %collective-permute-done.13 = f32[48,512]{1,0:T(8,128)S(1)} collective-permute-done((f32[48,512]{1,0:T(8,128)S(1)}, f32[48,512]{1,0:T(8,128)S(1)}, u32[]{:S(2)}, u32[]{:S(2)}) %collective-permute-start.13) | collective-permute-done | bytes 98336 | tf_op jit(solution)/shard_map/ppermute | solution.py:182
  61.4 1.1 collective-permute-done.14
  62.6 1.4 collective-permute-start.17
  63.9 1.5 collective-permute-start.15
  65.5 1.6 %collective-permute-start.16 = (f32[4,48,512]{2,1,0:T(8,128)S(1)}, f32[4,48,512]{2,1,0:T(8,128)S(1)}, u32[]{:S(2)}, u32[]{:S(2)}) collective-permute-start(f32[4,48,512]{2,1,0:T(8,128)S(1)} %get-tuple-element.30), channel_id=1, source_target_pairs={{0,128},{1,33},{2,130},{3,35},{4,132},{5,37},{6,134},{7,39},{8,136... | collective-permute-start | bytes 1179656 | tf_op jit(solution)/shard_map/ppermute | solution.py:182
  67.0 1.0 collective-permute-start.4
  68.0 1.7 %collective-permute-start.5 = (f32[48,1024]{1,0:T(8,128)}, f32[48,1024]{1,0:T(8,128)}, u32[]{:S(2)}, u32[]{:S(2)}) collective-permute-start(f32[48,1024]{1,0:T(8,128)} %collective-permute-done.3.refs_4_), channel_id=1, source_target_pairs={{0,14},{1,15},{2,0},{3,1},{4,2},{5,3},{6,4},{7,5},{8,6},{9,7},{10,... | collective-permute-start | bytes 589832 | tf_op jit(solution)/shard_map/ppermute | solution.py:177
  69.7 1.1 collective-permute-done.17
  70.8 3.6 %collective-permute-done.15 = f32[4,48,512]{2,1,0:T(8,128)S(1)} collective-permute-done((f32[4,48,512]{2,1,0:T(8,128)S(1)}, f32[4,48,512]{2,1,0:T(8,128)S(1)}, u32[]{:S(2)}, u32[]{:S(2)}) %collective-permute-start.15) | collective-permute-done | bytes 393248 | tf_op jit(solution)/shard_map/ppermute | solution.py:182
  74.4 1.8 %collective-permute-done.16 = f32[4,48,512]{2,1,0:T(8,128)S(1)} collective-permute-done((f32[4,48,512]{2,1,0:T(8,128)S(1)}, f32[4,48,512]{2,1,0:T(8,128)S(1)}, u32[]{:S(2)}, u32[]{:S(2)}) %collective-permute-start.16) | collective-permute-done | bytes 393248 | tf_op jit(solution)/shard_map/ppermute | solution.py:182
  76.2 1.3 pad_maximum_fusion
  77.5 2.0 %collective-permute-start.18 = (f32[16,48,512]{2,1,0:T(8,128)}, f32[16,48,512]{2,1,0:T(8,128)}, u32[]{:S(2)}, u32[]{:S(2)}) collective-permute-start(f32[16,48,512]{2,1,0:T(8,128)} %bitcast.11.own_ref), channel_id=1, source_target_pairs={{0,1},{1,0},{2,3},{3,2},{4,5},{5,4},{6,7},{7,6},{8,9},{9,8},{10,11... | collective-permute-start | bytes 4718600 | tf_op jit(solution)/shard_map/ppermute | solution.py:177
  80.4 7.2 %all-to-all-start.1 = ((f32[16,8,8,128]{3,2,1,0:T(8,128)}), f32[16,8,8,128]{3,2,1,0:T(8,128)}, u32[]{:S(2)}, u32[]{:S(2)}) async-start(f32[16,8,8,128]{3,2,1,0:T(8,128)} %copy-done.5), calls=%async_computation.1 | async-start | bytes 1048576 | tf_op jit(solution)/shard_map/all_to_all | solution.py:188
  87.6 1.5 collective-permute-start.6
  89.1 0.9 slice.20
  90.0 1.3 collective-permute-start.7
  91.2 13.1 %collective-permute-done.6.refs_7_ = f32[24,1024]{1,0:T(8,128)S(1)} collective-permute-done((f32[24,1024]{1,0:T(8,128)S(1)}, f32[24,1024]{1,0:T(8,128)S(1)}, u32[]{:S(2)}, u32[]{:S(2)}) %collective-permute-start.6) | collective-permute-done | bytes 98336 | tf_op jit(solution)/shard_map/ppermute | solution.py:177
  105.8 1.1 copy-done.2
  106.9 5.5 %all-to-all-start = ((f32[16,8,24,128]{3,2,1,0:T(8,128)}), f32[16,8,24,128]{3,2,1,0:T(8,128)}, u32[]{:S(2)}, u32[]{:S(2)}) async-start(f32[16,8,24,128]{3,2,1,0:T(8,128)} %copy-done.2), calls=%async_computation | async-start | bytes 3145728 | tf_op jit(solution)/shard_map/all_to_all | solution.py:188
  112.5 1.1 copy-done.8
  113.6 1.1 copy-done.10
  115.6 6.1 %shard_map.38.own_ref = f32[8,48,1024]{2,1,0:T(8,128)S(1)} custom-call(f32[16,48,512]{2,1,0:T(8,128)} %bitcast.11.own_ref, f32[16,48,512]{2,1,0:T(8,128)} %collective-permute-done.18.other_ref, f32[48,1024]{1,0:T(8,128)S(1)} %slice.18.refs_0_, f32[48,1024]{1,0:T(8,128)S(1)} %copy-done.8, f32[48,1024]{1,0:T(8,128)} %collective-permute-done.1.refs_2_, ...), custom_call_target="tpu_custom_call" | custom-call | flops 3623878656 | bytes 6291456 | tf_op jit(solution)/shard_map/pallas_call | solution.py:77
  122.0 3.3 %collective-permute-done.19.other_ref = f32[8,48,1024]{2,1,0:T(8,128)S(1)} collective-permute-done((f32[8,48,1024]{2,1,0:T(8,128)S(1)}, f32[8,48,1024]{2,1,0:T(8,128)S(1)}, u32[]{:S(2)}, u32[]{:S(2)}) %collective-permute-start.19) | collective-permute-done | bytes 1572896 | tf_op jit(solution)/shard_map/ppermute | solution.py:177
  125.2 6.3 %shard_map.39.p_ref = f32[16,48,1024]{2,1,0:T(8,128)S(1)} custom-call(f32[8,48,1024]{2,1,0:T(8,128)S(1)} %shard_map.38.own_ref, f32[8,48,1024]{2,1,0:T(8,128)S(1)} %collective-permute-done.19.other_ref, f32[2,1,512,1024]{3,2,1,0:T(8,128)S(1)} %copy-done.6), custom_call_target="tpu_custom_call" | custom-call | flops 4831838208 | bytes 10485760 | tf_op jit(solution)/shard_map/pallas_call | solution.py:121
  131.5 1.9 %shard_map.43.rest_0_ = f32[16,384,128]{2,1,0:T(8,128)} custom-call(f32[16,8,8,128]{3,2,1,0:T(8,128)} %all-to-all-done.3.w_ref, f32[16,48,1024]{2,1,0:T(8,128)S(1)} %shard_map.39.p_ref), custom_call_target="tpu_custom_call" | custom-call | flops 131072 | bytes 1572864 | tf_op jit(solution)/shard_map/pallas_call | solution.py:144
  133.4 1.9 %shard_map.44.rest_0_ = f32[16,384,128]{2,1,0:T(8,128)} custom-call(f32[16,8,8,128]{3,2,1,0:T(8,128)} %all-to-all-done.2.w_ref, f32[16,48,1024]{2,1,0:T(8,128)S(1)} %shard_map.39.p_ref, f32[16,384,128]{2,1,0:T(8,128)} %shard_map.43.rest_0_), custom_call_target="tpu_custom_call", output_to_operand_aliasing={{}: (2, {})} | custom-call | flops 131072 | bytes 1572864 | tf_op jit(solution)/shard_map/pallas_call | solution.py:144
  135.4 1.9 %shard_map.45.rest_0_ = f32[16,384,128]{2,1,0:T(8,128)} custom-call(f32[16,8,8,128]{3,2,1,0:T(8,128)} %all-to-all-done.1.w_ref, f32[16,48,1024]{2,1,0:T(8,128)S(1)} %shard_map.39.p_ref, f32[16,384,128]{2,1,0:T(8,128)} %shard_map.44.rest_0_), custom_call_target="tpu_custom_call", output_to_operand_aliasing={{}: (2, {})} | custom-call | flops 131072 | bytes 1572864 | tf_op jit(solution)/shard_map/pallas_call | solution.py:144
  137.3 13.7 %all-to-all-done.w_ref = f32[16,8,24,128]{3,2,1,0:T(8,128)} async-done(((f32[16,8,24,128]{3,2,1,0:T(8,128)}), f32[16,8,24,128]{3,2,1,0:T(8,128)}, u32[]{:S(2)}, u32[]{:S(2)}) %all-to-all-start) | async-done | bytes 1572896 | tf_op jit(solution)/shard_map/all_to_all | solution.py:188
  151.0 2.8 %shard_map.46 = f32[16,384,128]{2,1,0:T(8,128)} custom-call(f32[16,8,24,128]{3,2,1,0:T(8,128)} %all-to-all-done.w_ref, f32[16,48,1024]{2,1,0:T(8,128)S(1)} %shard_map.39.p_ref, f32[16,384,128]{2,1,0:T(8,128)} %shard_map.45.rest_0_), custom_call_target="tpu_custom_call", output_to_operand_aliasing={{}: (2, {})} | custom-call | flops 393216 | bytes 4718592 | tf_op jit(solution)/shard_map/pallas_call | solution.py:144
  (50 shorter events, 8.3 us)
Async XLA Ops:
  0.9 11.1 %collective-permute-start = (f32[48,1024]{1,0:T(8,128)S(1)}, f32[48,1024]{1,0:T(8,128)S(1)}, u32[]{:S(2)}, u32[]{:S(2)}) collective-permute-start(f32[48,1024]{1,0:T(8,128)S(1)} %slice.18.refs_0_), channel_id=1, source_target_pairs={{0,2},{1,3},{2,4},{3,5},{4,6},{5,7},{6,8},{7,9},{8,10},{9,11},{10,... | collective-permute-start | bytes 589832 | tf_op jit(solution)/shard_map/ppermute | solution.py:177
  3.5 8.6 %collective-permute-start.1 = (f32[48,1024]{1,0:T(8,128)S(1)}, f32[48,1024]{1,0:T(8,128)}, u32[]{:S(2)}, u32[]{:S(2)}) collective-permute-start(f32[48,1024]{1,0:T(8,128)S(1)} %slice.18.refs_0_), channel_id=1, source_target_pairs={{0,14},{1,15},{2,0},{3,1},{4,2},{5,3},{6,4},{7,5},{8,6},{9,7},{10,... | collective-permute-start | bytes 589832 | tf_op jit(solution)/shard_map/ppermute | solution.py:177
  12.1 28.0 %copy-start.7 = (f32[48,1024]{1,0:T(8,128)}, f32[48,1024]{1,0:T(8,128)S(1)}, u32[]{:S(2)}) copy-start(f32[48,1024]{1,0:T(8,128)S(1)} %collective-permute-done.refs_1_) | copy-start | bytes 589828
  12.1 2.0 %copy-start = (f32[48,16384]{1,0:T(8,128)S(1)}, f32[48,16384]{1,0:T(8,128)}, u32[]{:S(2)}) copy-start(f32[48,16384]{1,0:T(8,128)} %w_ref.3) | copy-start | bytes 9437188
  14.0 32.6 %copy-start.1 = (f32[48,16384]{1,0:T(8,128)S(1)}, f32[48,16384]{1,0:T(8,128)}, u32[]{:S(2)}) copy-start(f32[48,16384]{1,0:T(8,128)} %w_ref.3) | copy-start | bytes 9437188
  14.1 0.8 copy-start.3
  14.9 32.6 %all-to-all-start.3 = ((f32[16,8,8,128]{3,2,1,0:T(8,128)}), f32[16,8,8,128]{3,2,1,0:T(8,128)}, u32[]{:S(2)}, u32[]{:S(2)}) async-start(f32[16,8,8,128]{3,2,1,0:T(8,128)} %copy-done.3), calls=%async_computation.3 | async-start | bytes 1048576 | tf_op jit(solution)/shard_map/all_to_all | solution.py:188
  23.6 10.3 %collective-permute-start.8 = (f32[32,512]{1,0:T(8,128)}, f32[32,512]{1,0:T(8,128)}, u32[]{:S(2)}, u32[]{:S(2)}) collective-permute-start(f32[32,512]{1,0:T(8,128)} %dynamic-slice_bitcast_fusion), channel_id=1, source_target_pairs={{1,5},{17,21},{33,37},{49,53},{65,69},{81,85},{97,101},{113,117},{... | collective-permute-start | bytes 196616 | tf_op jit(solution)/shard_map/ppermute | solution.py:177
  28.4 6.4 %collective-permute-start.9 = (f32[32,512]{1,0:T(8,128)}, f32[32,512]{1,0:T(8,128)}, u32[]{:S(2)}, u32[]{:S(2)}) collective-permute-start(f32[32,512]{1,0:T(8,128)} %dynamic-slice_bitcast_fusion), channel_id=1, source_target_pairs={{1,13},{17,29},{33,45},{49,61},{65,77},{81,93},{97,109},{113,125},... | collective-permute-start | bytes 196616 | tf_op jit(solution)/shard_map/ppermute | solution.py:177
  36.3 16.2 %collective-permute-start.10 = (f32[32,512]{1,0:T(8,128)}, f32[32,512]{1,0:T(8,128)}, u32[]{:S(2)}, u32[]{:S(2)}) collective-permute-start(f32[32,512]{1,0:T(8,128)} %add_select_fusion), channel_id=1, source_target_pairs={{1,3},{5,7},{13,11},{17,19},{21,23},{29,27},{33,35},{37,39},{45,43... | collective-permute-start | bytes 196616 | tf_op jit(solution)/shard_map/ppermute | solution.py:177
  38.2 14.3 %collective-permute-start.11 = (f32[32,512]{1,0:T(8,128)}, f32[32,512]{1,0:T(8,128)}, u32[]{:S(2)}, u32[]{:S(2)}) collective-permute-start(f32[32,512]{1,0:T(8,128)} %add_select_fusion), channel_id=1, source_target_pairs={{1,15},{5,9},{17,31},{21,25},{33,47},{37,41},{49,63},{53,57},{65,7... | collective-permute-start | bytes 196616 | tf_op jit(solution)/shard_map/ppermute | solution.py:177
  40.1 5.8 %collective-permute-start.2 = (f32[48,1024]{1,0:T(8,128)S(1)}, f32[48,1024]{1,0:T(8,128)}, u32[]{:S(2)}, u32[]{:S(2)}) collective-permute-start(f32[48,1024]{1,0:T(8,128)S(1)} %collective-permute-done.refs_1_), channel_id=1, source_target_pairs={{0,2},{1,3},{2,4},{3,5},{4,6},{5,7},{6,8},{7,9},{8,10},{9,11},{10,... | collective-permute-start | bytes 589832 | tf_op jit(solution)/shard_map/ppermute | solution.py:177
  40.1 6.5 %collective-permute-start.3 = (f32[48,1024]{1,0:T(8,128)}, f32[48,1024]{1,0:T(8,128)}, u32[]{:S(2)}, u32[]{:S(2)}) collective-permute-start(f32[48,1024]{1,0:T(8,128)} %collective-permute-done.1.refs_2_), channel_id=1, source_target_pairs={{0,14},{1,15},{2,0},{3,1},{4,2},{5,3},{6,4},{7,5},{8,6},{9,7},{10,... | collective-permute-start | bytes 589832 | tf_op jit(solution)/shard_map/ppermute | solution.py:177
  45.9 6.6 %copy-start.14 = (f32[2,32,512]{2,1,0:T(8,128)S(1)}, f32[2,32,512]{2,1,0:T(8,128)}, u32[]{:S(2)}) copy-start(f32[2,32,512]{2,1,0:T(8,128)} %param.5) | copy-start | bytes 393220
  45.9 7.6 %copy-start.13 = (f32[16,512]{1,0:T(8,128)S(1)}, f32[16,512]{1,0:T(8,128)}, u32[]{:S(2)}) copy-start(f32[16,512]{1,0:T(8,128)} %select_bitcast_fusion) | copy-start | bytes 98308
  46.7 0.8 copy-start.4
  47.5 32.9 %all-to-all-start.2 = ((f32[16,8,8,128]{3,2,1,0:T(8,128)}), f32[16,8,8,128]{3,2,1,0:T(8,128)}, u32[]{:S(2)}, u32[]{:S(2)}) async-start(f32[16,8,8,128]{3,2,1,0:T(8,128)} %copy-done.4), calls=%async_computation.2 | async-start | bytes 1048576 | tf_op jit(solution)/shard_map/all_to_all | solution.py:188
  53.5 4.2 %collective-permute-start.12 = (f32[48,512]{1,0:T(8,128)S(1)}, f32[48,512]{1,0:T(8,128)S(1)}, u32[]{:S(2)}, u32[]{:S(2)}) collective-permute-start(f32[48,512]{1,0:T(8,128)S(1)} %get-tuple-element.32), channel_id=1, source_target_pairs={{0,48},{1,193},{2,50},{3,195},{4,52},{5,197},{6,54},{7,199},{8,56}... | collective-permute-start | bytes 294920 | tf_op jit(solution)/shard_map/ppermute | solution.py:182
  56.1 5.4 %collective-permute-start.13 = (f32[48,512]{1,0:T(8,128)S(1)}, f32[48,512]{1,0:T(8,128)S(1)}, u32[]{:S(2)}, u32[]{:S(2)}) collective-permute-start(f32[48,512]{1,0:T(8,128)S(1)} %get-tuple-element.32), channel_id=1, source_target_pairs={{0,32},{1,129},{2,34},{3,131},{4,36},{5,133},{6,38},{7,135},{8,40}... | collective-permute-start | bytes 294920 | tf_op jit(solution)/shard_map/ppermute | solution.py:182
  56.6 5.9 %collective-permute-start.14 = (f32[48,512]{1,0:T(8,128)S(1)}, f32[48,512]{1,0:T(8,128)S(1)}, u32[]{:S(2)}, u32[]{:S(2)}) collective-permute-start(f32[48,512]{1,0:T(8,128)S(1)} %get-tuple-element.32), channel_id=1, source_target_pairs={{0,16},{1,65},{2,18},{3,67},{4,20},{5,69},{6,22},{7,71},{8,24},{9,... | collective-permute-start | bytes 294920 | tf_op jit(solution)/shard_map/ppermute | solution.py:182
  62.6 8.3 %collective-permute-start.17 = (f32[4,48,512]{2,1,0:T(8,128)S(1)}, f32[4,48,512]{2,1,0:T(8,128)S(1)}, u32[]{:S(2)}, u32[]{:S(2)}) collective-permute-start(f32[4,48,512]{2,1,0:T(8,128)S(1)} %get-tuple-element.30), channel_id=1, source_target_pairs={{0,64},{1,17},{2,66},{3,19},{4,68},{5,21},{6,70},{7,23},{8,72},{9,... | collective-permute-start | bytes 1179656 | tf_op jit(solution)/shard_map/ppermute | solution.py:182
  63.9 10.5 %collective-permute-start.15 = (f32[4,48,512]{2,1,0:T(8,128)S(1)}, f32[4,48,512]{2,1,0:T(8,128)S(1)}, u32[]{:S(2)}, u32[]{:S(2)}) collective-permute-start(f32[4,48,512]{2,1,0:T(8,128)S(1)} %get-tuple-element.30), channel_id=1, source_target_pairs={{0,192},{1,49},{2,194},{3,51},{4,196},{5,53},{6,198},{7,55},{8,200... | collective-permute-start | bytes 1179656 | tf_op jit(solution)/shard_map/ppermute | solution.py:182
  65.5 10.8 %collective-permute-start.16 = (f32[4,48,512]{2,1,0:T(8,128)S(1)}, f32[4,48,512]{2,1,0:T(8,128)S(1)}, u32[]{:S(2)}, u32[]{:S(2)}) collective-permute-start(f32[4,48,512]{2,1,0:T(8,128)S(1)} %get-tuple-element.30), channel_id=1, source_target_pairs={{0,128},{1,33},{2,130},{3,35},{4,132},{5,37},{6,134},{7,39},{8,136... | collective-permute-start | bytes 1179656 | tf_op jit(solution)/shard_map/ppermute | solution.py:182
  67.0 12.5 %collective-permute-start.4 = (f32[48,1024]{1,0:T(8,128)}, f32[48,1024]{1,0:T(8,128)S(1)}, u32[]{:S(2)}, u32[]{:S(2)}) collective-permute-start(f32[48,1024]{1,0:T(8,128)} %collective-permute-done.2.refs_3_), channel_id=1, source_target_pairs={{0,2},{1,3},{2,4},{3,5},{4,6},{5,7},{6,8},{7,9},{8,10},{9,11},{10,... | collective-permute-start | bytes 589832 | tf_op jit(solution)/shard_map/ppermute | solution.py:177
  68.0 11.6 %collective-permute-start.5 = (f32[48,1024]{1,0:T(8,128)}, f32[48,1024]{1,0:T(8,128)}, u32[]{:S(2)}, u32[]{:S(2)}) collective-permute-start(f32[48,1024]{1,0:T(8,128)} %collective-permute-done.3.refs_4_), channel_id=1, source_target_pairs={{0,14},{1,15},{2,0},{3,1},{4,2},{5,3},{6,4},{7,5},{8,6},{9,7},{10,... | collective-permute-start | bytes 589832 | tf_op jit(solution)/shard_map/ppermute | solution.py:177
  77.5 34.9 %collective-permute-start.18 = (f32[16,48,512]{2,1,0:T(8,128)}, f32[16,48,512]{2,1,0:T(8,128)}, u32[]{:S(2)}, u32[]{:S(2)}) collective-permute-start(f32[16,48,512]{2,1,0:T(8,128)} %bitcast.11.own_ref), channel_id=1, source_target_pairs={{0,1},{1,0},{2,3},{3,2},{4,5},{5,4},{6,7},{7,6},{8,9},{9,8},{10,11... | collective-permute-start | bytes 4718600 | tf_op jit(solution)/shard_map/ppermute | solution.py:177
  79.6 0.8 copy-start.5
  80.4 26.5 %all-to-all-start.1 = ((f32[16,8,8,128]{3,2,1,0:T(8,128)}), f32[16,8,8,128]{3,2,1,0:T(8,128)}, u32[]{:S(2)}, u32[]{:S(2)}) async-start(f32[16,8,8,128]{3,2,1,0:T(8,128)} %copy-done.5), calls=%async_computation.1 | async-start | bytes 1048576 | tf_op jit(solution)/shard_map/all_to_all | solution.py:188
  87.6 16.8 %collective-permute-start.6 = (f32[24,1024]{1,0:T(8,128)S(1)}, f32[24,1024]{1,0:T(8,128)S(1)}, u32[]{:S(2)}, u32[]{:S(2)}) collective-permute-start(f32[24,1024]{1,0:T(8,128)S(1)} %slice.19), channel_id=1, source_target_pairs={{0,2},{1,3},{2,4},{3,5},{4,6},{5,7},{6,8},{7,9},{8,10},{9,11},{10,... | collective-permute-start | bytes 294920 | tf_op jit(solution)/shard_map/ppermute | solution.py:177
  90.0 15.1 %collective-permute-start.7 = (f32[24,1024]{1,0:T(8,128)S(1)}, f32[24,1024]{1,0:T(8,128)S(1)}, u32[]{:S(2)}, u32[]{:S(2)}) collective-permute-start(f32[24,1024]{1,0:T(8,128)S(1)} %slice.20), channel_id=1, source_target_pairs={{0,14},{1,15},{2,0},{3,1},{4,2},{5,3},{6,4},{7,5},{8,6},{9,7},{10,... | collective-permute-start | bytes 294920 | tf_op jit(solution)/shard_map/ppermute | solution.py:177
  104.4 0.6 copy-start.9
  105.0 0.6 copy-start.11
  105.8 1.2 copy-start.2
  106.9 44.1 %all-to-all-start = ((f32[16,8,24,128]{3,2,1,0:T(8,128)}), f32[16,8,24,128]{3,2,1,0:T(8,128)}, u32[]{:S(2)}, u32[]{:S(2)}) async-start(f32[16,8,24,128]{3,2,1,0:T(8,128)} %copy-done.2), calls=%async_computation | async-start | bytes 3145728 | tf_op jit(solution)/shard_map/all_to_all | solution.py:188
  112.5 12.8 %copy-start.6 = (f32[2,1,512,1024]{3,2,1,0:T(8,128)S(1)}, f32[2,1,512,1024]{3,2,1,0:T(8,128)}, u32[]{:S(2)}) copy-start(f32[2,1,512,1024]{3,2,1,0:T(8,128)} %panel_ref.1) | copy-start | bytes 12582916
  112.5 1.1 copy-start.8
  113.6 1.2 copy-start.10
  114.7 0.9 copy-start.12
  121.7 3.5 %collective-permute-start.19 = (f32[8,48,1024]{2,1,0:T(8,128)S(1)}, f32[8,48,1024]{2,1,0:T(8,128)S(1)}, u32[]{:S(2)}, u32[]{:S(2)}) collective-permute-start(f32[8,48,1024]{2,1,0:T(8,128)S(1)} %shard_map.38.own_ref), channel_id=1, source_target_pairs={{0,1},{1,0},{2,3},{3,2},{4,5},{5,4},{6,7},{7,6},{8,9},{9,8},{10,11... | collective-permute-start | bytes 4718600 | tf_op jit(solution)/shard_map/ppermute | solution.py:177

commit v2 on v1

v2 whole, which is shorter than its diff:
```python
import functools

import jax
import jax.numpy as jnp
from jax import lax
from jax.experimental import pallas as pl
from jax.experimental.pallas import tpu as pltpu
from jax.sharding import PartitionSpec as P

B = 512
NT = (((1,), (1,)), ((), ()))
SIDE = 4
COST = pl.CostEstimate(flops=1024, bytes_accessed=1024, transcendentals=0)


def dot_exact(left, right):
    return lax.dot_general(left, right, NT, precision=lax.Precision.HIGHEST, preferred_element_type=jnp.float32)


def dot_half(left, right):
    return lax.dot_general(left, right, NT, preferred_element_type=jnp.float32)


def split(value):
    high = value.astype(jnp.bfloat16)
    return high, (value - high.astype(jnp.float32)).astype(jnp.bfloat16)


def pack_body(w_ref, o_ref):
    for c in range(16):
        for k in range(8):
            o_ref[c, k] = w_ref[:, pl.ds(((k // 4) * 16 + c) * B + (k % 4) * 128, 128)]


def pack(weight):
    return pl.pallas_call(
        pack_body,
        out_shape=jax.ShapeDtypeStruct((16, 8, 48, 128), jnp.float32),
        compiler_params=pltpu.CompilerParams(vmem_limit_bytes=8 << 20),
        cost_estimate=COST,
    )(weight)


def choose_body(slab_ref, inverse_ref, o_ref):
    even = lax.axis_index("cols") % 2 == 0
    o_ref[:32] = jnp.where(even, inverse_ref[0], slab_ref[...])
    o_ref[32:] = jnp.where(even, inverse_ref[1, :16], inverse_ref[1, 16:])


def choose(slab, inverse):
    return pl.pallas_call(
        choose_body,
        out_shape=jax.ShapeDtypeStruct((48, B), jnp.float32),
        compiler_params=pltpu.CompilerParams(vmem_limit_bytes=4 << 20),
        cost_estimate=pl.CostEstimate(flops=10**12, bytes_accessed=10**9, transcendentals=0),
    )(slab, inverse)


def solve_body(own_ref, other_ref, *refs):
    blocks, (x_ref, w_scr, d0_scr, d1_scr, l_scr) = refs[:9], refs[9:]
    r, c = lax.axis_index("rows"), lax.axis_index("cols")
    x, y, z, parity = r // 4, r % 4, c // 2, c % 2
    for q in range(16):
        dx, dy = (q // 4 - x + 4) % 4, (q % 4 - y + 4) % 4
        at_even, at_odd = dx * 4 + dy, dy * 4 + dx
        own = own_ref[jnp.where(parity == 0, at_even, at_odd)]
        other = other_ref[jnp.where(parity == 0, at_odd, at_even)]
        even = jnp.where(parity == 0, own, other)
        odd = jnp.where(parity == 0, other, own)
        d0_scr[32 * q : 32 * q + 32] = even[:32]
        l_scr[32 * q : 32 * q + 32] = odd[:32]
        d1_scr[32 * q : 32 * q + 16] = even[32:]
        d1_scr[32 * q + 16 : 32 * q + 32] = odd[32:]
    for i in range(7):
        w_scr[48 * i : 48 * i + 48] = blocks[i][...]
    w_scr[336:360] = blocks[7][...]
    w_scr[360:384] = blocks[8][...]
    first = dot_exact(w_scr[:, :B], d0_scr[...])
    second = dot_exact(w_scr[:, B:] - dot_exact(first, l_scr[...]), d1_scr[...])
    for i, shift in enumerate((0, 7, 1, 6, 2, 5, 3, 4)):
        at = (z + shift) % 8
        x_ref[at, :, :B] = first[48 * i : 48 * i + 48]
        x_ref[at, :, B:] = second[48 * i : 48 * i + 48]


def solve(own, other, blocks):
    return pl.pallas_call(
        solve_body,
        out_shape=jax.ShapeDtypeStruct((8, 48, 2 * B), jnp.float32),
        scratch_shapes=[
            pltpu.VMEM((384, 2 * B), jnp.float32),
            pltpu.VMEM((B, B), jnp.float32),
            pltpu.VMEM((B, B), jnp.float32),
            pltpu.VMEM((B, B), jnp.float32),
        ],
        compiler_params=pltpu.CompilerParams(vmem_limit_bytes=20 << 20),
        cost_estimate=COST,
    )(own, other, *blocks)


def product_body(own_ref, other_ref, panel_ref, out_ref, xh_scr, xl_scr, p_ref):
    c = lax.axis_index("cols")
    parity = c % 2
    for part, ref in ((parity, own_ref), (1 - parity, other_ref)):
        for z in range(8):
            value = ref[z]
            high, low = split(value)
            at = pl.multiple_of((2 * z + part) * 48, 16)
            xh_scr[pl.ds(at, 48)] = high
            xl_scr[pl.ds(at, 48)] = low

    def step(j, carry):
        h, i = j // 2, j % 2
        lh, ll = split(panel_ref[h, 0, pl.ds(pl.multiple_of(i * 256, 256), 256), :])
        out = dot_half(xh_scr[...], lh) + (dot_half(xl_scr[...], lh) + dot_half(xh_scr[...], ll))
        p_ref[:, :, pl.ds(pl.multiple_of(j * 256, 256), 256)] = out.reshape(16, 48, 256)
        return carry

    lax.fori_loop(0, 4, step, 0)

    for which in range(2):

        @pl.when(c == which)
        def _():
            for part, ref in ((parity, own_ref), (1 - parity, other_ref)):
                for z in range(8):
                    p_ref[2 * z + part, :, :B] = -ref[z, :, which * B : which * B + B]

    pltpu.sync_copy(p_ref, out_ref)


def product(own, other, panel):
    return pl.pallas_call(
        product_body,
        out_shape=jax.ShapeDtypeStruct((16, 48, 2 * B), jnp.float32),
        out_specs=pl.BlockSpec(memory_space=pltpu.HBM),
        scratch_shapes=[
            pltpu.VMEM((768, 2 * B), jnp.bfloat16),
            pltpu.VMEM((768, 2 * B), jnp.bfloat16),
            pltpu.VMEM((16, 48, 2 * B), jnp.float32),
        ],
        compiler_params=pltpu.CompilerParams(vmem_limit_bytes=24 << 20),
        cost_estimate=COST,
    )(own, other, panel)


def finish_body(w_ref, prod_ref, o_ref, p_scr, scr, in_sems, out_sems):
    solved = lax.axis_index("cols") < 2
    reads = [pltpu.make_async_copy(prod_ref.at[s], p_scr.at[s], in_sems.at[s]) for s in range(16)]
    writes = [pltpu.make_async_copy(scr.at[s], o_ref.at[s], out_sems.at[s]) for s in range(16)]
    for read in reads:
        read.start()
    for s in range(16):
        reads[s].wait()
        for k in range(8):
            w = w_ref[s, k]
            if k < 4:
                w = jnp.where(solved, jnp.zeros_like(w), w)
            scr[s, pl.ds(k, 48, stride=8), :] = w - p_scr[s, :, k * 128 : k * 128 + 128]
        writes[s].start()
    for write in writes:
        write.wait()


def finish(part, prod):
    return pl.pallas_call(
        finish_body,
        out_shape=jax.ShapeDtypeStruct((16, 384, 128), jnp.float32),
        in_specs=[pl.BlockSpec(memory_space=pltpu.VMEM), pl.BlockSpec(memory_space=pltpu.HBM)],
        out_specs=pl.BlockSpec(memory_space=pltpu.HBM),
        scratch_shapes=[
            pltpu.VMEM((16, 48, 2 * B), jnp.float32),
            pltpu.VMEM((16, 384, 128), jnp.float32),
            pltpu.SemaphoreType.DMA((16,)),
            pltpu.SemaphoreType.DMA((16,)),
        ],
        compiler_params=pltpu.CompilerParams(vmem_limit_bytes=16 << 20),
        cost_estimate=COST,
    )(part, prod)


def plane_shift(amount, first_phase):
    pairs = []
    for x in range(SIDE):
        for y in range(SIDE):
            for c in range(16):
                along_y = first_phase == (c % 2 == 0)
                tx, ty = (x, (y + amount) % SIDE) if along_y else ((x + amount) % SIDE, y)
                pairs.append(((x * SIDE + y) * 16 + c, (tx * SIDE + ty) * 16 + c))
    return pairs


UP = [(i, (i + 2) % 16) for i in range(16)]
DOWN = [(i, (i - 2) % 16) for i in range(16)]
UP2 = [(i, (i + 4) % 16) for i in range(16)]
DOWN2 = [(i, (i - 4) % 16) for i in range(16)]
TWIN = [(i, i ^ 1) for i in range(16)]


def along(value, pairs):
    return lax.ppermute(value, "cols", pairs)


def plane_step(value, phase):
    got = [lax.ppermute(value, ("rows", "cols"), plane_shift(a, phase)) for a in (-1, 2, 1)]
    return jnp.stack([value] + got)


def tie(*values):
    return lax.optimization_barrier(values)


def exchange(part):
    return lax.all_to_all(part, "cols", split_axis=0, concat_axis=0, tiled=True)


def per_device(weight, factor_panel, diag_inverse):
    r, c = lax.axis_index("rows"), lax.axis_index("cols")

    lead = weight[:, : 2 * B]
    slab = lax.dynamic_slice(factor_panel, (0, 0, r * 32, 0), (1, 1, 32, B))[0, 0]

    def hand(slab, pairs):
        targets = functools.reduce(jnp.logical_or, [c == to for _, to in pairs])
        return jnp.where(targets, along(slab, pairs), slab)

    slab = hand(hand(slab, [(1, 9)]), [(1, 5), (9, 13)])
    up2, down2 = along(lead, UP2), along(lead, DOWN2)
    up1, down1 = along(lead, UP), along(lead, DOWN)
    up2, down2, slab, packed = tie(up2, down2, slab, pack(weight))
    slab = hand(slab, [(1, 3), (5, 7), (9, 11), (13, 15)])
    up3, down3 = along(up2, UP), along(down2, DOWN)
    up4, down4 = along(up2[:24], UP2), along(down2[24:], DOWN2)
    packed, slab, up1, down1 = tie(packed, slab, up1, down1)
    part = exchange(packed)
    slab, *blocks = tie(slab, lead, up1, down1, up2, down2, up3, down3, up4, down4)
    half = choose(slab, diag_inverse)
    row = plane_step(half, True)
    own = plane_step(row, False).reshape(16, 48, B)
    other = along(own, TWIN)
    mine = solve(own, other, blocks)
    theirs = along(mine, TWIN)
    prod = product(mine, theirs, factor_panel)
    return finish(part, prod).reshape(768, 2, 1, B)


def solution(mesh):
    placed = (P(("rows", "cols"), None), P(None, "cols", None, None), P(None, "rows", None))
    return jax.shard_map(
        per_device,
        mesh=mesh,
        in_specs=placed,
        out_specs=P("rows", None, "cols", None),
        check_vma=False,
    )
```

time: 155 us -> 121 us (0.78)
  starting transfers between devices: 61.1 us -> 40 us
  local copies, waits for them, and re-layouts: 13.2 us -> 3.7 us
  other arithmetic: 5.26 us -> 1.1 us
  waiting for transfers between devices: 52.8 us -> 54.8 us
    all_to_all x4 -> x1, starting transfers between devices: 25 us -> 4.38 us  [exchange(): return lax.all_to_all(part, 'cols', split_axis=0, concat_axis=0, tiled=True)]
    all_to_all x4 -> x1, waiting for transfers between devices: 13.7 us -> 30.3 us  [exchange(): return lax.all_to_all(part, 'cols', split_axis=0, concat_axis=0, tiled=True)]
    ppermute x14 -> x13, waiting for transfers between devices: 27.3 us -> 13 us  [along(): return lax.ppermute(value, 'cols', pairs)]
    unnamed x30 -> x6, local copies, waits for them, and re-layouts: 9.89 us -> 1.9 us
    select_n x3, other arithmetic: 3.87 us -> 0.87 us  [hand(): return jnp.where(targets, along(slab, pairs), slab)]
    pallas_call x1, Pallas kernels: 6.13 us -> 4.09 us  [solve(): pl.pallas_call(solve_body, out_shape=jax.ShapeDtypeStruct((8, 48, 2 * B),...]
    ppermute x14 -> x13, starting transfers between devices: 28 us -> 26.2 us  [along(): return lax.ppermute(value, 'cols', pairs)]
    pallas_call x8 -> x3, Pallas kernels: 8.82 us -> 9.75 us  [the longest x1 7.86 us: finish(): pl.pallas_call(finish_body, out_shape=jax.ShapeDtypeStruct((16, 384, 128)...]
  transfers between devices with their start and end apart: 24 -> 20, of which waited for: 14 -> 13; matrix products, arithmetic and copies ran while one was open for 5% -> 1% of each run, Pallas kernels for 12% -> 10%
where the time goes in v2:
time: 121 us; the launch traced here: 120 us
  waiting for transfers between devices  54.8 us (45%)
  starting transfers between devices  40 us (33%)
  Pallas kernels  20.3 us (17%)
  local copies, waits for them, and re-layouts  3.7 us (3%)
    all_to_all x1, waiting for transfers between devices, exchange(): return lax.all_to_all(part, 'cols', split_axis=0, concat_axis=0, tiled=True)  30.3 us
    ppermute x13, starting transfers between devices, along(): return lax.ppermute(value, 'cols', pairs)  26.2 us
    ppermute x13, waiting for transfers between devices, along(): return lax.ppermute(value, 'cols', pairs)  13 us
    ppermute x6, waiting for transfers between devices, plane_step(): lax.ppermute(value, ('rows', 'cols'), plane_shift(a, phase))  11.5 us
    ppermute x6, starting transfers between devices, plane_step(): lax.ppermute(value, ('rows', 'cols'), plane_shift(a, phase))  9.36 us
    pallas_call x1, Pallas kernels, finish(): pl.pallas_call(finish_body, out_shape=jax.ShapeDtypeStruct((16, 384, 128)...  7.86 us
    pallas_call x1, Pallas kernels, product(): pl.pallas_call(product_body, out_shape=jax.ShapeDtypeStruct((16, 48, 2 *...  6.5 us
    all_to_all x1, starting transfers between devices, exchange(): return lax.all_to_all(part, 'cols', split_axis=0, concat_axis=0, tiled=True)  4.38 us
  transfers between devices with their start and end apart: 20, of which 13 were waited for; matrix products, arithmetic and copies ran while one was open for 1% of the time, Pallas kernels for 10%

profile of v2, /device:TPU:1, one launch (start us, length us, event | category | flops | bytes accessed | tf_op | source)
XLA Modules:
  0.0 120.3 jit_solution(6920169926777161914)
XLA Ops:
  0.0 0.8 dynamic-slice_bitcast_fusion
  0.8 9.6 %collective-permute-start.2 = (f32[32,512]{1,0:T(8,128)S(1)}, f32[32,512]{1,0:T(8,128)S(1)}, u32[]{:S(2)}, u32[]{:S(2)}) collective-permute-start(f32[32,512]{1,0:T(8,128)S(1)} %dynamic-slice_bitcast_fusion), channel_id=1, source_target_pairs={{1,9},{17,25},{33,41},{49,57},{65,73},{81,89},{97,105},{113,121},{... | collective-permute-start | bytes 196616 | tf_op jit(solution)/shard_map/ppermute | solution.py:201
  10.5 1.3 %collective-permute-done.2 = f32[32,512]{1,0:T(8,128)S(1)} collective-permute-done((f32[32,512]{1,0:T(8,128)S(1)}, f32[32,512]{1,0:T(8,128)S(1)}, u32[]{:S(2)}, u32[]{:S(2)}) %collective-permute-start.2) | collective-permute-done | bytes 65568 | tf_op jit(solution)/shard_map/ppermute | solution.py:201
  11.8 0.8 broadcast_select_fusion.1
  12.7 1.3 %collective-permute-start.3 = (f32[32,512]{1,0:T(8,128)S(1)}, f32[32,512]{1,0:T(8,128)S(1)}, u32[]{:S(2)}, u32[]{:S(2)}) collective-permute-start(f32[32,512]{1,0:T(8,128)S(1)} %broadcast_select_fusion.1), channel_id=1, source_target_pairs={{1,5},{9,13},{17,21},{25,29},{33,37},{41,45},{49,53},{57,61},{65,6... | collective-permute-start | bytes 196616 | tf_op jit(solution)/shard_map/ppermute | solution.py:201
  14.0 0.9 slice.9.refs_0_
  14.9 0.1 collective-permute-start.6
  15.0 0.1 collective-permute-start.1
  15.1 2.4 %collective-permute-start = (f32[48,1024]{1,0:T(8,128)S(1)}, f32[48,1024]{1,0:T(8,128)S(1)}, u32[]{:S(2)}, u32[]{:S(2)}) collective-permute-start(f32[48,1024]{1,0:T(8,128)S(1)} %slice.9.refs_0_), channel_id=1, source_target_pairs={{0,4},{1,5},{2,6},{3,7},{4,8},{5,9},{6,10},{7,11},{8,12},{9,13},{1... | collective-permute-start | bytes 589832 | tf_op jit(solution)/shard_map/ppermute | solution.py:201
  17.4 1.9 %copy-done.1 = f32[48,16384]{1,0:T(8,128)S(1)} copy-done((f32[48,16384]{1,0:T(8,128)S(1)}, f32[48,16384]{1,0:T(8,128)}, u32[]{:S(2)}) %copy-start.1) | copy-done | bytes 3145752
  19.3 1.9 %shard_map.37 = f32[16,8,48,128]{3,2,1,0:T(8,128)} custom-call(f32[48,16384]{1,0:T(8,128)S(1)} %copy-done.1), custom_call_target="tpu_custom_call" | custom-call | flops 1024 | bytes 1024 | tf_op jit(solution)/shard_map/pallas_call | solution.py:36
  21.2 0.0 collective-permute-done.3
  21.2 2.2 %collective-permute-done.1.refs_4_ = f32[48,1024]{1,0:T(8,128)S(1)} collective-permute-done((f32[48,1024]{1,0:T(8,128)S(1)}, f32[48,1024]{1,0:T(8,128)S(1)}, u32[]{:S(2)}, u32[]{:S(2)}) %collective-permute-start.1) | collective-permute-done | bytes 196640 | tf_op jit(solution)/shard_map/ppermute | solution.py:201
  23.4 0.8 collective-permute-done.refs_3_
  24.2 5.2 %collective-permute-start.4 = (f32[32,512]{1,0:T(8,128)S(1)}, f32[32,512]{1,0:T(8,128)S(1)}, u32[]{:S(2)}, u32[]{:S(2)}) collective-permute-start(f32[32,512]{1,0:T(8,128)S(1)} %broadcast_select_fusion.2), channel_id=1, source_target_pairs={{1,3},{5,7},{9,11},{13,15},{17,19},{21,23},{25,27},{29,31},{33,35}... | collective-permute-start | bytes 196616 | tf_op jit(solution)/shard_map/ppermute | solution.py:201
  29.4 0.1 collective-permute-start.5
  29.5 2.6 %collective-permute-start.7 = (f32[48,1024]{1,0:T(8,128)S(1)}, f32[48,1024]{1,0:T(8,128)S(1)}, u32[]{:S(2)}, u32[]{:S(2)}) collective-permute-start(f32[48,1024]{1,0:T(8,128)S(1)} %collective-permute-done.refs_3_), channel_id=1, source_target_pairs={{0,2},{1,3},{2,4},{3,5},{4,6},{5,7},{6,8},{7,9},{8,10},{9,11},{10,... | collective-permute-start | bytes 589832 | tf_op jit(solution)/shard_map/ppermute | solution.py:201
  32.1 0.3 collective-permute-start.8
  32.4 1.2 %collective-permute-start.10 = (f32[24,1024]{1,0:T(8,128)S(1)}, f32[24,1024]{1,0:T(8,128)S(1)}, u32[]{:S(2)}, u32[]{:S(2)}) collective-permute-start(f32[24,1024]{1,0:T(8,128)S(1)} %slice.11), channel_id=1, source_target_pairs={{0,12},{1,13},{2,14},{3,15},{4,0},{5,1},{6,2},{7,3},{8,4},{9,5},{1... | collective-permute-start | bytes 294920 | tf_op jit(solution)/shard_map/ppermute | solution.py:201
  33.6 1.1 collective-permute-start.9
  34.8 0.0 copy-start.2
  34.8 2.6 %collective-permute-done.5.refs_1_ = f32[48,1024]{1,0:T(8,128)S(1)} collective-permute-done((f32[48,1024]{1,0:T(8,128)S(1)}, f32[48,1024]{1,0:T(8,128)S(1)}, u32[]{:S(2)}, u32[]{:S(2)}) %collective-permute-start.5) | collective-permute-done | bytes 196640 | tf_op jit(solution)/shard_map/ppermute | solution.py:201
  37.3 4.4 %all-to-all-start = ((f32[16,8,48,128]{3,2,1,0:T(8,128)}), f32[16,8,48,128]{3,2,1,0:T(8,128)}, u32[]{:S(2)}, u32[]{:S(2)}) async-start(f32[16,8,48,128]{3,2,1,0:T(8,128)} %shard_map.37), calls=%async_computation | async-start | bytes 6291456 | tf_op jit(solution)/shard_map/all_to_all | solution.py:214
  41.7 0.0 collective-permute-done.10.refs_8_
  41.7 0.1 collective-permute-done.9.refs_7_
  41.8 0.0 collective-permute-done.7.refs_5_
  41.9 1.3 %collective-permute-start.13 = (f32[48,512]{1,0:T(8,128)S(1)}, f32[48,512]{1,0:T(8,128)S(1)}, u32[]{:S(2)}, u32[]{:S(2)}) collective-permute-start(f32[48,512]{1,0:T(8,128)S(1)} %shard_map.38), channel_id=1, source_target_pairs={{0,16},{1,65},{2,18},{3,67},{4,20},{5,69},{6,22},{7,71},{8,24},{9,... | collective-permute-start | bytes 294920 | tf_op jit(solution)/shard_map/ppermute | solution.py:205
  43.1 2.5 %collective-permute-start.12 = (f32[48,512]{1,0:T(8,128)S(1)}, f32[48,512]{1,0:T(8,128)S(1)}, u32[]{:S(2)}, u32[]{:S(2)}) collective-permute-start(f32[48,512]{1,0:T(8,128)S(1)} %shard_map.38), channel_id=1, source_target_pairs={{0,32},{1,129},{2,34},{3,131},{4,36},{5,133},{6,38},{7,135},{8,40}... | collective-permute-start | bytes 294920 | tf_op jit(solution)/shard_map/ppermute | solution.py:205
  45.6 1.2 collective-permute-start.11
  46.8 0.3 collective-permute-done.13
  47.0 2.0 %collective-permute-done.12 = f32[48,512]{1,0:T(8,128)S(1)} collective-permute-done((f32[48,512]{1,0:T(8,128)S(1)}, f32[48,512]{1,0:T(8,128)S(1)}, u32[]{:S(2)}, u32[]{:S(2)}) %collective-permute-start.12) | collective-permute-done | bytes 98336 | tf_op jit(solution)/shard_map/ppermute | solution.py:205
  49.1 0.4 collective-permute-done.11
  49.5 0.1 fusion
  49.5 3.0 %collective-permute-start.15 = (f32[4,48,512]{2,1,0:T(8,128)S(1)}, f32[4,48,512]{2,1,0:T(8,128)S(1)}, u32[]{:S(2)}, u32[]{:S(2)}) collective-permute-start(f32[4,48,512]{2,1,0:T(8,128)S(1)} %get-tuple-element.42), channel_id=1, source_target_pairs={{0,128},{1,33},{2,130},{3,35},{4,132},{5,37},{6,134},{7,39},{8,136... | collective-permute-start | bytes 1179656 | tf_op jit(solution)/shard_map/ppermute | solution.py:205
  52.5 0.8 collective-permute-start.14
  53.3 0.7 collective-permute-start.16
  54.0 4.2 %collective-permute-done.15 = f32[4,48,512]{2,1,0:T(8,128)S(1)} collective-permute-done((f32[4,48,512]{2,1,0:T(8,128)S(1)}, f32[4,48,512]{2,1,0:T(8,128)S(1)}, u32[]{:S(2)}, u32[]{:S(2)}) %collective-permute-start.15) | collective-permute-done | bytes 393248 | tf_op jit(solution)/shard_map/ppermute | solution.py:205
  58.1 4.6 %collective-permute-done.14 = f32[4,48,512]{2,1,0:T(8,128)S(1)} collective-permute-done((f32[4,48,512]{2,1,0:T(8,128)S(1)}, f32[4,48,512]{2,1,0:T(8,128)S(1)}, u32[]{:S(2)}, u32[]{:S(2)}) %collective-permute-start.14) | collective-permute-done | bytes 393248 | tf_op jit(solution)/shard_map/ppermute | solution.py:205
  62.7 0.0 collective-permute-done.16
  62.7 0.2 pad_maximum_fusion
  62.9 1.9 %collective-permute-start.17 = (f32[16,48,512]{2,1,0:T(8,128)S(1)}, f32[16,48,512]{2,1,0:T(8,128)S(1)}, u32[]{:S(2)}, u32[]{:S(2)}) collective-permute-start(f32[16,48,512]{2,1,0:T(8,128)S(1)} %bitcast.15), channel_id=1, source_target_pairs={{0,1},{1,0},{2,3},{3,2},{4,5},{5,4},{6,7},{7,6},{8,9},{9,8},{10,11... | collective-permute-start | bytes 4718600 | tf_op jit(solution)/shard_map/ppermute | solution.py:201
  64.8 3.0 %collective-permute-done.17.other_ref = f32[16,48,512]{2,1,0:T(8,128)S(1)} collective-permute-done((f32[16,48,512]{2,1,0:T(8,128)S(1)}, f32[16,48,512]{2,1,0:T(8,128)S(1)}, u32[]{:S(2)}, u32[]{:S(2)}) %collective-permute-start.17) | collective-permute-done | bytes 1572896 | tf_op jit(solution)/shard_map/ppermute | solution.py:201
  67.8 4.1 %shard_map.39.own_ref = f32[8,48,1024]{2,1,0:T(8,128)S(1)} custom-call(f32[16,48,512]{2,1,0:T(8,128)S(1)} %bitcast.16, f32[16,48,512]{2,1,0:T(8,128)S(1)} %collective-permute-done.17.other_ref, f32[48,1024]{1,0:T(8,128)S(1)} %slice.9.refs_0_, f32[48,1024]{1,0:T(8,128)S(1)} %collective-permute-done.5.refs_1_, f32[48,1024]{1,0:T(8,128)S(1)} %collective-permute-done.6.refs_2_, ...), custom_call_target="tpu_custom_call" | custom-call | flops 1024 | bytes 1024 | tf_op jit(solution)/shard_map/pallas_call | solution.py:87
  71.9 0.5 collective-permute-start.18
  72.4 3.0 %collective-permute-done.18.other_ref = f32[8,48,1024]{2,1,0:T(8,128)S(1)} collective-permute-done((f32[8,48,1024]{2,1,0:T(8,128)S(1)}, f32[8,48,1024]{2,1,0:T(8,128)S(1)}, u32[]{:S(2)}, u32[]{:S(2)}) %collective-permute-start.18) | collective-permute-done | bytes 1572896 | tf_op jit(solution)/shard_map/ppermute | solution.py:201
  75.4 6.5 %shard_map.40.prod_ref = f32[16,48,1024]{2,1,0:T(8,128)S(1)} custom-call(f32[8,48,1024]{2,1,0:T(8,128)S(1)} %shard_map.39.own_ref, f32[8,48,1024]{2,1,0:T(8,128)S(1)} %collective-permute-done.18.other_ref, f32[2,1,512,1024]{3,2,1,0:T(8,128)S(1)} %copy-done), custom_call_target="tpu_custom_call" | custom-call | flops 1024 | bytes 1024 | tf_op jit(solution)/shard_map/pallas_call | solution.py:133
  81.9 30.3 %all-to-all-done.w_ref = f32[16,8,48,128]{3,2,1,0:T(8,128)} async-done(((f32[16,8,48,128]{3,2,1,0:T(8,128)}), f32[16,8,48,128]{3,2,1,0:T(8,128)}, u32[]{:S(2)}, u32[]{:S(2)}) %all-to-all-start) | async-done | bytes 3145760 | tf_op jit(solution)/shard_map/all_to_all | solution.py:214
  112.2 7.9 %shard_map.41 = f32[16,384,128]{2,1,0:T(8,128)} custom-call(f32[16,8,48,128]{3,2,1,0:T(8,128)} %all-to-all-done.w_ref, f32[16,48,1024]{2,1,0:T(8,128)S(1)} %shard_map.40.prod_ref), custom_call_target="tpu_custom_call" | custom-call | flops 1024 | bytes 1024 | tf_op jit(solution)/shard_map/pallas_call | solution.py:166
  (12 shorter events, 0.1 us)
Async XLA Ops:
  0.8 11.0 %collective-permute-start.2 = (f32[32,512]{1,0:T(8,128)S(1)}, f32[32,512]{1,0:T(8,128)S(1)}, u32[]{:S(2)}, u32[]{:S(2)}) collective-permute-start(f32[32,512]{1,0:T(8,128)S(1)} %dynamic-slice_bitcast_fusion), channel_id=1, source_target_pairs={{1,9},{17,25},{33,41},{49,57},{65,73},{81,89},{97,105},{113,121},{... | collective-permute-start | bytes 196616 | tf_op jit(solution)/shard_map/ppermute | solution.py:201
  12.7 8.5 %collective-permute-start.3 = (f32[32,512]{1,0:T(8,128)S(1)}, f32[32,512]{1,0:T(8,128)S(1)}, u32[]{:S(2)}, u32[]{:S(2)}) collective-permute-start(f32[32,512]{1,0:T(8,128)S(1)} %broadcast_select_fusion.1), channel_id=1, source_target_pairs={{1,5},{9,13},{17,21},{25,29},{33,37},{41,45},{49,53},{57,61},{65,6... | collective-permute-start | bytes 196616 | tf_op jit(solution)/shard_map/ppermute | solution.py:201
  14.9 17.5 %collective-permute-start.6 = (f32[48,1024]{1,0:T(8,128)S(1)}, f32[48,1024]{1,0:T(8,128)S(1)}, u32[]{:S(2)}, u32[]{:S(2)}) collective-permute-start(f32[48,1024]{1,0:T(8,128)S(1)} %slice.9.refs_0_), channel_id=1, source_target_pairs={{0,14},{1,15},{2,0},{3,1},{4,2},{5,3},{6,4},{7,5},{8,6},{9,7},{10,... | collective-permute-start | bytes 589832 | tf_op jit(solution)/shard_map/ppermute | solution.py:201
  15.0 8.5 %collective-permute-start.1 = (f32[48,1024]{1,0:T(8,128)S(1)}, f32[48,1024]{1,0:T(8,128)S(1)}, u32[]{:S(2)}, u32[]{:S(2)}) collective-permute-start(f32[48,1024]{1,0:T(8,128)S(1)} %slice.9.refs_0_), channel_id=1, source_target_pairs={{0,12},{1,13},{2,14},{3,15},{4,0},{5,1},{6,2},{7,3},{8,4},{9,5},{1... | collective-permute-start | bytes 589832 | tf_op jit(solution)/shard_map/ppermute | solution.py:201
  15.1 9.1 %collective-permute-start = (f32[48,1024]{1,0:T(8,128)S(1)}, f32[48,1024]{1,0:T(8,128)S(1)}, u32[]{:S(2)}, u32[]{:S(2)}) collective-permute-start(f32[48,1024]{1,0:T(8,128)S(1)} %slice.9.refs_0_), channel_id=1, source_target_pairs={{0,4},{1,5},{2,6},{3,7},{4,8},{5,9},{6,10},{7,11},{8,12},{9,13},{1... | collective-permute-start | bytes 589832 | tf_op jit(solution)/shard_map/ppermute | solution.py:201
  17.4 1.9 %copy-start.1 = (f32[48,16384]{1,0:T(8,128)S(1)}, f32[48,16384]{1,0:T(8,128)}, u32[]{:S(2)}) copy-start(f32[48,16384]{1,0:T(8,128)} %w_ref.1) | copy-start | bytes 9437188
  24.2 9.4 %collective-permute-start.4 = (f32[32,512]{1,0:T(8,128)S(1)}, f32[32,512]{1,0:T(8,128)S(1)}, u32[]{:S(2)}, u32[]{:S(2)}) collective-permute-start(f32[32,512]{1,0:T(8,128)S(1)} %broadcast_select_fusion.2), channel_id=1, source_target_pairs={{1,3},{5,7},{9,11},{13,15},{17,19},{21,23},{25,27},{29,31},{33,35}... | collective-permute-start | bytes 196616 | tf_op jit(solution)/shard_map/ppermute | solution.py:201
  29.4 7.9 %collective-permute-start.5 = (f32[48,1024]{1,0:T(8,128)S(1)}, f32[48,1024]{1,0:T(8,128)S(1)}, u32[]{:S(2)}, u32[]{:S(2)}) collective-permute-start(f32[48,1024]{1,0:T(8,128)S(1)} %slice.9.refs_0_), channel_id=1, source_target_pairs={{0,2},{1,3},{2,4},{3,5},{4,6},{5,7},{6,8},{7,9},{8,10},{9,11},{10,... | collective-permute-start | bytes 589832 | tf_op jit(solution)/shard_map/ppermute | solution.py:201
  29.5 12.3 %collective-permute-start.7 = (f32[48,1024]{1,0:T(8,128)S(1)}, f32[48,1024]{1,0:T(8,128)S(1)}, u32[]{:S(2)}, u32[]{:S(2)}) collective-permute-start(f32[48,1024]{1,0:T(8,128)S(1)} %collective-permute-done.refs_3_), channel_id=1, source_target_pairs={{0,2},{1,3},{2,4},{3,5},{4,6},{5,7},{6,8},{7,9},{8,10},{9,11},{10,... | collective-permute-start | bytes 589832 | tf_op jit(solution)/shard_map/ppermute | solution.py:201
  32.1 9.7 %collective-permute-start.8 = (f32[48,1024]{1,0:T(8,128)S(1)}, f32[48,1024]{1,0:T(8,128)S(1)}, u32[]{:S(2)}, u32[]{:S(2)}) collective-permute-start(f32[48,1024]{1,0:T(8,128)S(1)} %collective-permute-done.1.refs_4_), channel_id=1, source_target_pairs={{0,14},{1,15},{2,0},{3,1},{4,2},{5,3},{6,4},{7,5},{8,6},{9,7},{10,... | collective-permute-start | bytes 589832 | tf_op jit(solution)/shard_map/ppermute | solution.py:201
  32.4 9.3 %collective-permute-start.10 = (f32[24,1024]{1,0:T(8,128)S(1)}, f32[24,1024]{1,0:T(8,128)S(1)}, u32[]{:S(2)}, u32[]{:S(2)}) collective-permute-start(f32[24,1024]{1,0:T(8,128)S(1)} %slice.11), channel_id=1, source_target_pairs={{0,12},{1,13},{2,14},{3,15},{4,0},{5,1},{6,2},{7,3},{8,4},{9,5},{1... | collective-permute-start | bytes 294920 | tf_op jit(solution)/shard_map/ppermute | solution.py:201
  33.6 8.2 %collective-permute-start.9 = (f32[24,1024]{1,0:T(8,128)S(1)}, f32[24,1024]{1,0:T(8,128)S(1)}, u32[]{:S(2)}, u32[]{:S(2)}) collective-permute-start(f32[24,1024]{1,0:T(8,128)S(1)} %slice.10), channel_id=1, source_target_pairs={{0,4},{1,5},{2,6},{3,7},{4,8},{5,9},{6,10},{7,11},{8,12},{9,13},{1... | collective-permute-start | bytes 294920 | tf_op jit(solution)/shard_map/ppermute | solution.py:201
  34.8 7.1 %copy-start.2 = (f32[2,32,512]{2,1,0:T(8,128)S(1)}, f32[2,32,512]{2,1,0:T(8,128)}, u32[]{:S(2)}) copy-start(f32[2,32,512]{2,1,0:T(8,128)} %inverse_ref.1) | copy-start | bytes 393220
  37.3 74.9 %all-to-all-start = ((f32[16,8,48,128]{3,2,1,0:T(8,128)}), f32[16,8,48,128]{3,2,1,0:T(8,128)}, u32[]{:S(2)}, u32[]{:S(2)}) async-start(f32[16,8,48,128]{3,2,1,0:T(8,128)} %shard_map.37), calls=%async_computation | async-start | bytes 6291456 | tf_op jit(solution)/shard_map/all_to_all | solution.py:214
  41.9 5.2 %collective-permute-start.13 = (f32[48,512]{1,0:T(8,128)S(1)}, f32[48,512]{1,0:T(8,128)S(1)}, u32[]{:S(2)}, u32[]{:S(2)}) collective-permute-start(f32[48,512]{1,0:T(8,128)S(1)} %shard_map.38), channel_id=1, source_target_pairs={{0,16},{1,65},{2,18},{3,67},{4,20},{5,69},{6,22},{7,71},{8,24},{9,... | collective-permute-start | bytes 294920 | tf_op jit(solution)/shard_map/ppermute | solution.py:205
  43.1 5.9 %collective-permute-start.12 = (f32[48,512]{1,0:T(8,128)S(1)}, f32[48,512]{1,0:T(8,128)S(1)}, u32[]{:S(2)}, u32[]{:S(2)}) collective-permute-start(f32[48,512]{1,0:T(8,128)S(1)} %shard_map.38), channel_id=1, source_target_pairs={{0,32},{1,129},{2,34},{3,131},{4,36},{5,133},{6,38},{7,135},{8,40}... | collective-permute-start | bytes 294920 | tf_op jit(solution)/shard_map/ppermute | solution.py:205
  45.6 3.9 %collective-permute-start.11 = (f32[48,512]{1,0:T(8,128)S(1)}, f32[48,512]{1,0:T(8,128)S(1)}, u32[]{:S(2)}, u32[]{:S(2)}) collective-permute-start(f32[48,512]{1,0:T(8,128)S(1)} %shard_map.38), channel_id=1, source_target_pairs={{0,48},{1,193},{2,50},{3,195},{4,52},{5,197},{6,54},{7,199},{8,56}... | collective-permute-start | bytes 294920 | tf_op jit(solution)/shard_map/ppermute | solution.py:205
  49.5 8.6 %collective-permute-start.15 = (f32[4,48,512]{2,1,0:T(8,128)S(1)}, f32[4,48,512]{2,1,0:T(8,128)S(1)}, u32[]{:S(2)}, u32[]{:S(2)}) collective-permute-start(f32[4,48,512]{2,1,0:T(8,128)S(1)} %get-tuple-element.42), channel_id=1, source_target_pairs={{0,128},{1,33},{2,130},{3,35},{4,132},{5,37},{6,134},{7,39},{8,136... | collective-permute-start | bytes 1179656 | tf_op jit(solution)/shard_map/ppermute | solution.py:205
  52.5 10.2 %collective-permute-start.14 = (f32[4,48,512]{2,1,0:T(8,128)S(1)}, f32[4,48,512]{2,1,0:T(8,128)S(1)}, u32[]{:S(2)}, u32[]{:S(2)}) collective-permute-start(f32[4,48,512]{2,1,0:T(8,128)S(1)} %get-tuple-element.42), channel_id=1, source_target_pairs={{0,192},{1,49},{2,194},{3,51},{4,196},{5,53},{6,198},{7,55},{8,200... | collective-permute-start | bytes 1179656 | tf_op jit(solution)/shard_map/ppermute | solution.py:205
  53.3 9.4 %collective-permute-start.16 = (f32[4,48,512]{2,1,0:T(8,128)S(1)}, f32[4,48,512]{2,1,0:T(8,128)S(1)}, u32[]{:S(2)}, u32[]{:S(2)}) collective-permute-start(f32[4,48,512]{2,1,0:T(8,128)S(1)} %get-tuple-element.42), channel_id=1, source_target_pairs={{0,64},{1,17},{2,66},{3,19},{4,68},{5,21},{6,70},{7,23},{8,72},{9,... | collective-permute-start | bytes 1179656 | tf_op jit(solution)/shard_map/ppermute | solution.py:205
  62.9 4.9 %collective-permute-start.17 = (f32[16,48,512]{2,1,0:T(8,128)S(1)}, f32[16,48,512]{2,1,0:T(8,128)S(1)}, u32[]{:S(2)}, u32[]{:S(2)}) collective-permute-start(f32[16,48,512]{2,1,0:T(8,128)S(1)} %bitcast.15), channel_id=1, source_target_pairs={{0,1},{1,0},{2,3},{3,2},{4,5},{5,4},{6,7},{7,6},{8,9},{9,8},{10,11... | collective-permute-start | bytes 4718600 | tf_op jit(solution)/shard_map/ppermute | solution.py:201
  67.8 7.6 %copy-start = (f32[2,1,512,1024]{3,2,1,0:T(8,128)S(1)}, f32[2,1,512,1024]{3,2,1,0:T(8,128)}, u32[]{:S(2)}) copy-start(f32[2,1,512,1024]{3,2,1,0:T(8,128)} %panel_ref.1) | copy-start | bytes 12582916
  71.9 3.5 %collective-permute-start.18 = (f32[8,48,1024]{2,1,0:T(8,128)S(1)}, f32[8,48,1024]{2,1,0:T(8,128)S(1)}, u32[]{:S(2)}, u32[]{:S(2)}) collective-permute-start(f32[8,48,1024]{2,1,0:T(8,128)S(1)} %shard_map.39.own_ref), channel_id=1, source_target_pairs={{0,1},{1,0},{2,3},{3,2},{4,5},{5,4},{6,7},{7,6},{8,9},{9,8},{10,11... | collective-permute-start | bytes 4718600 | tf_op jit(solution)/shard_map/ppermute | solution.py:201

commit v3 on v2

--- a/solution.py
+++ b/solution.py
@@ -10,6 +10,7 @@
 B = 512
 NT = (((1,), (1,)), ((), ()))
 SIDE = 4
+HEAVY = pl.CostEstimate(flops=10**12, bytes_accessed=10**9, transcendentals=0)
 COST = pl.CostEstimate(flops=1024, bytes_accessed=1024, transcendentals=0)
 
 
@@ -41,23 +42,57 @@
     )(weight)
 
 
-def choose_body(slab_ref, inverse_ref, o_ref):
-    even = lax.axis_index("cols") % 2 == 0
-    o_ref[:32] = jnp.where(even, inverse_ref[0], slab_ref[...])
+def slab_body(panel_ref, o_ref):
+    r = lax.axis_index("rows")
+    pltpu.sync_copy(panel_ref.at[0, 0, pl.ds(pl.multiple_of(r * 32, 32), 32), pl.ds(0, B)], o_ref)
+
+
+def take_slab(panel):
+    return pl.pallas_call(
+        slab_body,
+        out_shape=jax.ShapeDtypeStruct((32, B), jnp.float32),
+        in_specs=[pl.BlockSpec(memory_space=pl.ANY)],
+        compiler_params=pltpu.CompilerParams(vmem_limit_bytes=4 << 20),
+        cost_estimate=HEAVY,
+    )(panel)
+
+
+def merge_body(targets, own_ref, *refs):
+    c = lax.axis_index("cols")
+    value = own_ref[...]
+    for to, ref in zip(targets, refs):
+        value = jnp.where(c == to, ref[...], value)
+    refs[-1][...] = value
+
+
+def merge(own, targets, got):
+    return pl.pallas_call(
+        functools.partial(merge_body, targets),
+        out_shape=jax.ShapeDtypeStruct(own.shape, own.dtype),
+        compiler_params=pltpu.CompilerParams(vmem_limit_bytes=4 << 20),
+        cost_estimate=HEAVY,
+    )(own, *got)
+
+
+def choose_body(slab_ref, got_ref, inverse_ref, o_ref):
+    c = lax.axis_index("cols")
+    even = c % 2 == 0
+    slab = jnp.where(c % 4 == 1, slab_ref[...], got_ref[...])
+    o_ref[:32] = jnp.where(even, inverse_ref[0], slab)
     o_ref[32:] = jnp.where(even, inverse_ref[1, :16], inverse_ref[1, 16:])
 
 
-def choose(slab, inverse):
+def choose(slab, got, inverse):
     return pl.pallas_call(
         choose_body,
         out_shape=jax.ShapeDtypeStruct((48, B), jnp.float32),
         compiler_params=pltpu.CompilerParams(vmem_limit_bytes=4 << 20),
-        cost_estimate=pl.CostEstimate(flops=10**12, bytes_accessed=10**9, transcendentals=0),
-    )(slab, inverse)
+        cost_estimate=HEAVY,
+    )(slab, got, inverse)
 
 
 def solve_body(own_ref, other_ref, *refs):
-    blocks, (x_ref, w_scr, d0_scr, d1_scr, l_scr) = refs[:9], refs[9:]
+    blocks, (x_ref, w_scr, d0_scr, d1_scr, l_scr) = refs[:8], refs[8:]
     r, c = lax.axis_index("rows"), lax.axis_index("cols")
     x, y, z, parity = r // 4, r % 4, c // 2, c % 2
     for q in range(16):
@@ -71,10 +106,8 @@
         l_scr[32 * q : 32 * q + 32] = odd[:32]
         d1_scr[32 * q : 32 * q + 16] = even[32:]
         d1_scr[32 * q + 16 : 32 * q + 32] = odd[32:]
-    for i in range(7):
+    for i in range(8):
         w_scr[48 * i : 48 * i + 48] = blocks[i][...]
-    w_scr[336:360] = blocks[7][...]
-    w_scr[360:384] = blocks[8][...]
     first = dot_exact(w_scr[:, :B], d0_scr[...])
     second = dot_exact(w_scr[:, B:] - dot_exact(first, l_scr[...]), d1_scr[...])
     for i, shift in enumerate((0, 7, 1, 6, 2, 5, 3, 4)):
@@ -98,7 +131,7 @@
     )(own, other, *blocks)
 
 
-def product_body(own_ref, other_ref, panel_ref, out_ref, xh_scr, xl_scr, p_ref):
+def product_body(own_ref, other_ref, panel_ref, p_ref, xh_scr, xl_scr):
     c = lax.axis_index("cols")
     parity = c % 2
     for part, ref in ((parity, own_ref), (1 - parity, other_ref)):
@@ -126,37 +159,33 @@
                 for z in range(8):
                     p_ref[2 * z + part, :, :B] = -ref[z, :, which * B : which * B + B]
 
-    pltpu.sync_copy(p_ref, out_ref)
-
 
 def product(own, other, panel):
     return pl.pallas_call(
         product_body,
         out_shape=jax.ShapeDtypeStruct((16, 48, 2 * B), jnp.float32),
-        out_specs=pl.BlockSpec(memory_space=pltpu.HBM),
         scratch_shapes=[
             pltpu.VMEM((768, 2 * B), jnp.bfloat16),
             pltpu.VMEM((768, 2 * B), jnp.bfloat16),
-            pltpu.VMEM((16, 48, 2 * B), jnp.float32),
         ],
         compiler_params=pltpu.CompilerParams(vmem_limit_bytes=24 << 20),
         cost_estimate=COST,
     )(own, other, panel)
 
 
-def finish_body(w_ref, prod_ref, o_ref, p_scr, scr, in_sems, out_sems):
+def finish_body(part_ref, p_ref, o_ref, w_scr, scr, in_sems, out_sems):
     solved = lax.axis_index("cols") < 2
-    reads = [pltpu.make_async_copy(prod_ref.at[s], p_scr.at[s], in_sems.at[s]) for s in range(16)]
+    reads = [pltpu.make_async_copy(part_ref.at[s], w_scr.at[s], in_sems.at[s]) for s in range(16)]
     writes = [pltpu.make_async_copy(scr.at[s], o_ref.at[s], out_sems.at[s]) for s in range(16)]
     for read in reads:
         read.start()
     for s in range(16):
         reads[s].wait()
         for k in range(8):
-            w = w_ref[s, k]
+            w = w_scr[s, k]
             if k < 4:
                 w = jnp.where(solved, jnp.zeros_like(w), w)
-            scr[s, pl.ds(k, 48, stride=8), :] = w - p_scr[s, :, k * 128 : k * 128 + 128]
+            scr[s, pl.ds(k, 48, stride=8), :] = w - p_ref[s, :, k * 128 : k * 128 + 128]
         writes[s].start()
     for write in writes:
         write.wait()
@@ -166,10 +195,10 @@
     return pl.pallas_call(
         finish_body,
         out_shape=jax.ShapeDtypeStruct((16, 384, 128), jnp.float32),
-        in_specs=[pl.BlockSpec(memory_space=pltpu.VMEM), pl.BlockSpec(memory_space=pltpu.HBM)],
-        out_specs=pl.BlockSpec(memory_space=pltpu.HBM),
+        in_specs=[pl.BlockSpec(memory_space=pl.ANY), pl.BlockSpec(memory_space=pltpu.VMEM)],
+        out_specs=pl.BlockSpec(memory_space=pl.ANY),
         scratch_shapes=[
-            pltpu.VMEM((16, 48, 2 * B), jnp.float32),
+            pltpu.VMEM((16, 8, 48, 128), jnp.float32),
             pltpu.VMEM((16, 384, 128), jnp.float32),
             pltpu.SemaphoreType.DMA((16,)),
             pltpu.SemaphoreType.DMA((16,)),
@@ -194,6 +223,7 @@
 DOWN = [(i, (i - 2) % 16) for i in range(16)]
 UP2 = [(i, (i + 4) % 16) for i in range(16)]
 DOWN2 = [(i, (i - 4) % 16) for i in range(16)]
+SPLIT2 = [(i, (i + (4 if i % 2 == 0 else 12)) % 16) for i in range(16)]
 TWIN = [(i, i ^ 1) for i in range(16)]
 
 
@@ -215,26 +245,20 @@
 
 
 def per_device(weight, factor_panel, diag_inverse):
-    r, c = lax.axis_index("rows"), lax.axis_index("cols")
-
     lead = weight[:, : 2 * B]
-    slab = lax.dynamic_slice(factor_panel, (0, 0, r * 32, 0), (1, 1, 32, B))[0, 0]
-
-    def hand(slab, pairs):
-        targets = functools.reduce(jnp.logical_or, [c == to for _, to in pairs])
-        return jnp.where(targets, along(slab, pairs), slab)
-
-    slab = hand(hand(slab, [(1, 9)]), [(1, 5), (9, 13)])
+    up1, down1 = along(lead, UP), along(lead, DOWN)
     up2, down2 = along(lead, UP2), along(lead, DOWN2)
-    up1, down1 = along(lead, UP), along(lead, DOWN)
-    up2, down2, slab, packed = tie(up2, down2, slab, pack(weight))
-    slab = hand(slab, [(1, 3), (5, 7), (9, 11), (13, 15)])
+    packed, panel = tie(pack(weight), factor_panel)
+    slab = take_slab(panel)
+    first, up1, down1 = tie([along(slab, [(1, to)]) for to in (5, 9, 13)], up1, down1)
+    slab = merge(slab, (5, 9, 13), first)
+    got = along(slab, [(1, 3), (5, 7), (9, 11), (13, 15)])
     up3, down3 = along(up2, UP), along(down2, DOWN)
-    up4, down4 = along(up2[:24], UP2), along(down2[24:], DOWN2)
-    packed, slab, up1, down1 = tie(packed, slab, up1, down1)
+    opposite = along(jnp.where(lax.axis_index("cols") % 2 == 0, up2, down2), SPLIT2)
+    packed, slab = tie(packed, slab)
     part = exchange(packed)
-    slab, *blocks = tie(slab, lead, up1, down1, up2, down2, up3, down3, up4, down4)
-    half = choose(slab, diag_inverse)
+    slab, got, *blocks = tie(slab, got, lead, up1, down1, up2, down2, up3, down3, opposite)
+    half = choose(slab, got, diag_inverse)
     row = plane_step(half, True)
     own = plane_step(row, False).reshape(16, 48, B)
     other = along(own, TWIN)

time: 121 us -> 110 us (0.909)
  waiting for transfers between devices: 54.8 us -> 45.1 us
  Pallas kernels: 20.3 us -> 17 us
  starting transfers between devices: 40 us -> 41.5 us
    all_to_all x1, waiting for transfers between devices: 30.3 us -> 25.2 us  [exchange(): return lax.all_to_all(part, 'cols', split_axis=0, concat_axis=0, tiled=True)]
    pallas_call x1, Pallas kernels: 7.86 us -> 3.12 us  [finish(): pl.pallas_call(finish_body, out_shape=jax.ShapeDtypeStruct((16, 384, 128)...]
    ppermute x13, waiting for transfers between devices: 13 us -> 8.43 us  [along(): return lax.ppermute(value, 'cols', pairs)]
    pallas_call x1, Pallas kernels: 4.09 us -> 5.67 us  [solve(): pl.pallas_call(solve_body, out_shape=jax.ShapeDtypeStruct((8, 48, 2 * B),...]
    ppermute x13, starting transfers between devices: 26.2 us -> 27.7 us  [along(): return lax.ppermute(value, 'cols', pairs)]
  transfers between devices with their start and end apart: 20 -> 20, of which waited for: 13 -> 11; matrix products, arithmetic and copies ran while one was open for 1% -> 2% of each run, Pallas kernels for 10% -> 13%
where the time goes in v3:
time: 110 us; the launch traced here: 109 us
  waiting for transfers between devices  45.1 us (41%)
  starting transfers between devices  41.5 us (38%)
  Pallas kernels  17 us (15%)
  local copies, waits for them, and re-layouts  3.51 us (3%)
  other arithmetic  1.88 us (2%)
    ppermute x13, starting transfers between devices, along(): return lax.ppermute(value, 'cols', pairs)  27.7 us
    all_to_all x1, waiting for transfers between devices, exchange(): return lax.all_to_all(part, 'cols', split_axis=0, concat_axis=0, tiled=True)  25.2 us
    ppermute x6, waiting for transfers between devices, plane_step(): lax.ppermute(value, ('rows', 'cols'), plane_shift(a, phase))  11.5 us
    ppermute x6, starting transfers between devices, plane_step(): lax.ppermute(value, ('rows', 'cols'), plane_shift(a, phase))  9.36 us
    ppermute x13, waiting for transfers between devices, along(): return lax.ppermute(value, 'cols', pairs)  8.43 us
    pallas_call x1, Pallas kernels, product(): pl.pallas_call(product_body, out_shape=jax.ShapeDtypeStruct((16, 48, 2 *...  6.26 us
    pallas_call x1, Pallas kernels, solve(): pl.pallas_call(solve_body, out_shape=jax.ShapeDtypeStruct((8, 48, 2 * B),...  5.67 us
    all_to_all x1, starting transfers between devices, exchange(): return lax.all_to_all(part, 'cols', split_axis=0, concat_axis=0, tiled=True)  4.45 us
  transfers between devices with their start and end apart: 20, of which 11 were waited for; matrix products, arithmetic and copies ran while one was open for 2% of the time, Pallas kernels for 13%

profile of v3, /device:TPU:1, one launch (start us, length us, event | category | flops | bytes accessed | tf_op | source)
XLA Modules:
  0.0 109.3 jit_solution(5973669237987850241)
XLA Ops:
  0.0 1.6 %slice.3.refs_0_ = f32[48,1024]{1,0:T(8,128)} slice(f32[48,16384]{1,0:T(8,128)} %w_ref.1), slice={[0:48], [0:1024]} | slice | bytes 393216 | tf_op jit(solution)/shard_map/slice | solution.py:248
  1.6 6.8 %collective-permute-start.7 = (f32[48,1024]{1,0:T(8,128)}, f32[48,1024]{1,0:T(8,128)}, u32[]{:S(2)}, u32[]{:S(2)}) collective-permute-start(f32[48,1024]{1,0:T(8,128)} %slice.3.refs_0_), channel_id=1, source_target_pairs={{0,12},{1,13},{2,14},{3,15},{4,0},{5,1},{6,2},{7,3},{8,4},{9,5},{1... | collective-permute-start | bytes 589832 | tf_op jit(solution)/shard_map/ppermute | solution.py:231
  8.5 0.0 collective-permute-start.6
  8.5 3.1 %collective-permute-start.4 = (f32[48,1024]{1,0:T(8,128)}, f32[48,1024]{1,0:T(8,128)}, u32[]{:S(2)}, u32[]{:S(2)}) collective-permute-start(f32[48,1024]{1,0:T(8,128)} %slice.3.refs_0_), channel_id=1, source_target_pairs={{0,14},{1,15},{2,0},{3,1},{4,2},{5,3},{6,4},{7,5},{8,6},{9,7},{10,... | collective-permute-start | bytes 589832 | tf_op jit(solution)/shard_map/ppermute | solution.py:231
  11.6 0.0 collective-permute-start.3
  11.6 1.9 %copy-done.2 = f32[48,16384]{1,0:T(8,128)S(1)} copy-done((f32[48,16384]{1,0:T(8,128)S(1)}, f32[48,16384]{1,0:T(8,128)}, u32[]{:S(2)}) %copy-start.2) | copy-done | bytes 3145752
  13.5 1.9 %shard_map.37 = f32[16,8,48,128]{3,2,1,0:T(8,128)} custom-call(f32[48,16384]{1,0:T(8,128)S(1)} %copy-done.2), custom_call_target="tpu_custom_call" | custom-call | flops 1024 | bytes 1024 | tf_op jit(solution)/shard_map/pallas_call | solution.py:37
  15.4 3.8 %collective-permute-start.2 = (f32[32,512]{1,0:T(8,128)S(1)}, f32[32,512]{1,0:T(8,128)S(1)}, u32[]{:S(2)}, u32[]{:S(2)}) collective-permute-start(f32[32,512]{1,0:T(8,128)S(1)} %shard_map.38.own_ref), channel_id=1, source_target_pairs={{1,13},{17,29},{33,45},{49,61},{65,77},{81,93},{97,109},{113,125},... | collective-permute-start | bytes 196616 | tf_op jit(solution)/shard_map/ppermute | solution.py:231
  19.2 0.0 collective-permute-done.7.refs_4_
  19.2 3.3 %collective-permute-start.1 = (f32[32,512]{1,0:T(8,128)S(1)}, f32[32,512]{1,0:T(8,128)S(1)}, u32[]{:S(2)}, u32[]{:S(2)}) collective-permute-start(f32[32,512]{1,0:T(8,128)S(1)} %shard_map.38.own_ref), channel_id=1, source_target_pairs={{1,9},{17,25},{33,41},{49,57},{65,73},{81,89},{97,105},{113,121},{... | collective-permute-start | bytes 196616 | tf_op jit(solution)/shard_map/ppermute | solution.py:231
  22.6 0.0 collective-permute-done.6.refs_3_
  22.6 1.3 %collective-permute-start = (f32[32,512]{1,0:T(8,128)S(1)}, f32[32,512]{1,0:T(8,128)S(1)}, u32[]{:S(2)}, u32[]{:S(2)}) collective-permute-start(f32[32,512]{1,0:T(8,128)S(1)} %shard_map.38.own_ref), channel_id=1, source_target_pairs={{1,5},{17,21},{33,37},{49,53},{65,69},{81,85},{97,101},{113,117},{... | collective-permute-start | bytes 196616 | tf_op jit(solution)/shard_map/ppermute | solution.py:231
  23.9 1.7 %broadcast_select_fusion = f32[48,1024]{1,0:T(8,128)} fusion(f32[48,1024]{1,0:T(8,128)} %collective-permute-done.6.refs_3_, f32[48,1024]{1,0:T(8,128)} %collective-permute-done.7.refs_4_, pred[]{:T(512)S(6)} %eq.5), kind=kLoop, calls=%fused_computation.2 | loop fusion | flops 49152 | bytes 589825 | tf_op jit(solution)/shard_map/jit(_where)/select_n | solution.py:257
  25.5 0.0 collective-permute-done.2.refs_2_
  25.5 1.0 collective-permute-start.10
  26.5 0.0 collective-permute-done.1.refs_1_
  26.5 0.0 collective-permute-done.3.refs_1_
  26.5 0.1 collective-permute-start.9
  26.6 1.5 %collective-permute-start.8 = (f32[48,1024]{1,0:T(8,128)}, f32[48,1024]{1,0:T(8,128)}, u32[]{:S(2)}, u32[]{:S(2)}) collective-permute-start(f32[48,1024]{1,0:T(8,128)} %collective-permute-done.6.refs_3_), channel_id=1, source_target_pairs={{0,2},{1,3},{2,4},{3,5},{4,6},{5,7},{6,8},{7,9},{8,10},{9,11},{10,... | collective-permute-start | bytes 589832 | tf_op jit(solution)/shard_map/ppermute | solution.py:231
  28.1 0.0 copy-start.3
  28.1 2.3 %collective-permute-start.5 = (f32[32,512]{1,0:T(8,128)S(1)}, f32[32,512]{1,0:T(8,128)S(1)}, u32[]{:S(2)}, u32[]{:S(2)}) collective-permute-start(f32[32,512]{1,0:T(8,128)S(1)} %shard_map.39.slab_ref), channel_id=1, source_target_pairs={{1,3},{5,7},{9,11},{13,15},{17,19},{21,23},{25,27},{29,31},{33,35}... | collective-permute-start | bytes 196616 | tf_op jit(solution)/shard_map/ppermute | solution.py:231
  30.4 4.4 %all-to-all-start = ((f32[16,8,48,128]{3,2,1,0:T(8,128)}), f32[16,8,48,128]{3,2,1,0:T(8,128)}, u32[]{:S(2)}, u32[]{:S(2)}) async-start(f32[16,8,48,128]{3,2,1,0:T(8,128)} %shard_map.37), calls=%async_computation | async-start | bytes 6291456 | tf_op jit(solution)/shard_map/all_to_all | solution.py:244
  34.9 0.9 collective-permute-done.5.got_ref
  35.8 0.1 collective-permute-done.9.refs_6_
  35.9 0.0 collective-permute-done.10.refs_7_
  35.9 1.3 %collective-permute-done.8.refs_5_ = f32[48,1024]{1,0:T(8,128)} collective-permute-done((f32[48,1024]{1,0:T(8,128)}, f32[48,1024]{1,0:T(8,128)}, u32[]{:S(2)}, u32[]{:S(2)}) %collective-permute-start.8) | collective-permute-done | bytes 196640 | tf_op jit(solution)/shard_map/ppermute | solution.py:231
  37.3 1.3 %collective-permute-start.13 = (f32[48,512]{1,0:T(8,128)S(1)}, f32[48,512]{1,0:T(8,128)S(1)}, u32[]{:S(2)}, u32[]{:S(2)}) collective-permute-start(f32[48,512]{1,0:T(8,128)S(1)} %shard_map.40), channel_id=1, source_target_pairs={{0,16},{1,65},{2,18},{3,67},{4,20},{5,69},{6,22},{7,71},{8,24},{9,... | collective-permute-start | bytes 294920 | tf_op jit(solution)/shard_map/ppermute | solution.py:235
  38.5 2.5 %collective-permute-start.12 = (f32[48,512]{1,0:T(8,128)S(1)}, f32[48,512]{1,0:T(8,128)S(1)}, u32[]{:S(2)}, u32[]{:S(2)}) collective-permute-start(f32[48,512]{1,0:T(8,128)S(1)} %shard_map.40), channel_id=1, source_target_pairs={{0,32},{1,129},{2,34},{3,131},{4,36},{5,133},{6,38},{7,135},{8,40}... | collective-permute-start | bytes 294920 | tf_op jit(solution)/shard_map/ppermute | solution.py:235
  41.0 1.2 %collective-permute-start.11 = (f32[48,512]{1,0:T(8,128)S(1)}, f32[48,512]{1,0:T(8,128)S(1)}, u32[]{:S(2)}, u32[]{:S(2)}) collective-permute-start(f32[48,512]{1,0:T(8,128)S(1)} %shard_map.40), channel_id=1, source_target_pairs={{0,48},{1,193},{2,50},{3,195},{4,52},{5,197},{6,54},{7,199},{8,56}... | collective-permute-start | bytes 294920 | tf_op jit(solution)/shard_map/ppermute | solution.py:235
  42.2 0.3 collective-permute-done.13
  42.4 2.0 %collective-permute-done.12 = f32[48,512]{1,0:T(8,128)S(1)} collective-permute-done((f32[48,512]{1,0:T(8,128)S(1)}, f32[48,512]{1,0:T(8,128)S(1)}, u32[]{:S(2)}, u32[]{:S(2)}) %collective-permute-start.12) | collective-permute-done | bytes 98336 | tf_op jit(solution)/shard_map/ppermute | solution.py:235
  44.5 0.4 collective-permute-done.11
  44.9 0.1 fusion
  44.9 3.0 %collective-permute-start.15 = (f32[4,48,512]{2,1,0:T(8,128)S(1)}, f32[4,48,512]{2,1,0:T(8,128)S(1)}, u32[]{:S(2)}, u32[]{:S(2)}) collective-permute-start(f32[4,48,512]{2,1,0:T(8,128)S(1)} %get-tuple-element.44), channel_id=1, source_target_pairs={{0,128},{1,33},{2,130},{3,35},{4,132},{5,37},{6,134},{7,39},{8,136... | collective-permute-start | bytes 1179656 | tf_op jit(solution)/shard_map/ppermute | solution.py:235
  47.9 0.8 collective-permute-start.14
  48.7 0.7 collective-permute-start.16
  49.4 4.2 %collective-permute-done.15 = f32[4,48,512]{2,1,0:T(8,128)S(1)} collective-permute-done((f32[4,48,512]{2,1,0:T(8,128)S(1)}, f32[4,48,512]{2,1,0:T(8,128)S(1)}, u32[]{:S(2)}, u32[]{:S(2)}) %collective-permute-start.15) | collective-permute-done | bytes 393248 | tf_op jit(solution)/shard_map/ppermute | solution.py:235
  53.5 4.6 %collective-permute-done.14 = f32[4,48,512]{2,1,0:T(8,128)S(1)} collective-permute-done((f32[4,48,512]{2,1,0:T(8,128)S(1)}, f32[4,48,512]{2,1,0:T(8,128)S(1)}, u32[]{:S(2)}, u32[]{:S(2)}) %collective-permute-start.14) | collective-permute-done | bytes 393248 | tf_op jit(solution)/shard_map/ppermute | solution.py:235
  58.1 0.0 collective-permute-done.16
  58.1 0.2 pad_maximum_fusion
  58.3 4.0 %collective-permute-start.17 = (f32[16,48,512]{2,1,0:T(8,128)S(1)}, f32[16,48,512]{2,1,0:T(8,128)S(1)}, u32[]{:S(2)}, u32[]{:S(2)}) collective-permute-start(f32[16,48,512]{2,1,0:T(8,128)S(1)} %bitcast.11), channel_id=1, source_target_pairs={{0,1},{1,0},{2,3},{3,2},{4,5},{5,4},{6,7},{7,6},{8,9},{9,8},{10,11... | collective-permute-start | bytes 4718600 | tf_op jit(solution)/shard_map/ppermute | solution.py:231
  62.3 3.0 %collective-permute-done.17.other_ref = f32[16,48,512]{2,1,0:T(8,128)S(1)} collective-permute-done((f32[16,48,512]{2,1,0:T(8,128)S(1)}, f32[16,48,512]{2,1,0:T(8,128)S(1)}, u32[]{:S(2)}, u32[]{:S(2)}) %collective-permute-start.17) | collective-permute-done | bytes 1572896 | tf_op jit(solution)/shard_map/ppermute | solution.py:231
  65.3 5.7 %shard_map.41.own_ref = f32[8,48,1024]{2,1,0:T(8,128)S(1)} custom-call(f32[16,48,512]{2,1,0:T(8,128)S(1)} %bitcast.12, f32[16,48,512]{2,1,0:T(8,128)S(1)} %collective-permute-done.17.other_ref, f32[48,1024]{1,0:T(8,128)} %slice.3.refs_0_, f32[48,1024]{1,0:T(8,128)} %collective-permute-done.3.refs_1_, f32[48,1024]{1,0:T(8,128)} %collective-permute-done.4.refs_2_, ...), custom_call_target="tpu_custom_call" | custom-call | flops 1024 | bytes 1024 | tf_op jit(solution)/shard_map/pallas_call | solution.py:120
  71.0 0.5 collective-permute-start.18
  71.5 3.0 %collective-permute-done.18.other_ref = f32[8,48,1024]{2,1,0:T(8,128)S(1)} collective-permute-done((f32[8,48,1024]{2,1,0:T(8,128)S(1)}, f32[8,48,1024]{2,1,0:T(8,128)S(1)}, u32[]{:S(2)}, u32[]{:S(2)}) %collective-permute-start.18) | collective-permute-done | bytes 1572896 | tf_op jit(solution)/shard_map/ppermute | solution.py:231
  74.5 6.3 %shard_map.42.p_ref = f32[16,48,1024]{2,1,0:T(8,128)S(1)} custom-call(f32[8,48,1024]{2,1,0:T(8,128)S(1)} %shard_map.41.own_ref, f32[8,48,1024]{2,1,0:T(8,128)S(1)} %collective-permute-done.18.other_ref, f32[2,1,512,1024]{3,2,1,0:T(8,128)S(1)} %copy-done.1), custom_call_target="tpu_custom_call" | custom-call | flops 1024 | bytes 1024 | tf_op jit(solution)/shard_map/pallas_call | solution.py:164
  80.8 25.2 %all-to-all-done.part_ref = f32[16,8,48,128]{3,2,1,0:T(8,128)} async-done(((f32[16,8,48,128]{3,2,1,0:T(8,128)}), f32[16,8,48,128]{3,2,1,0:T(8,128)}, u32[]{:S(2)}, u32[]{:S(2)}) %all-to-all-start) | async-done | bytes 3145760 | tf_op jit(solution)/shard_map/all_to_all | solution.py:244
  106.0 3.1 %shard_map.43 = f32[16,384,128]{2,1,0:T(8,128)} custom-call(f32[16,8,48,128]{3,2,1,0:T(8,128)} %all-to-all-done.part_ref, f32[16,48,1024]{2,1,0:T(8,128)S(1)} %shard_map.42.p_ref), custom_call_target="tpu_custom_call" | custom-call | flops 1024 | bytes 1024 | tf_op jit(solution)/shard_map/pallas_call | solution.py:195
  (11 shorter events, 0.1 us)
Async XLA Ops:
  1.6 13.7 %copy-start = (f32[2,1,512,1024]{3,2,1,0:T(8,128)S(1)}, f32[2,1,512,1024]{3,2,1,0:T(8,128)}, u32[]{:S(2)}) copy-start(f32[2,1,512,1024]{3,2,1,0:T(8,128)} %panel_ref.2) | copy-start | bytes 12582916
  1.6 17.6 %collective-permute-start.7 = (f32[48,1024]{1,0:T(8,128)}, f32[48,1024]{1,0:T(8,128)}, u32[]{:S(2)}, u32[]{:S(2)}) collective-permute-start(f32[48,1024]{1,0:T(8,128)} %slice.3.refs_0_), channel_id=1, source_target_pairs={{0,12},{1,13},{2,14},{3,15},{4,0},{5,1},{6,2},{7,3},{8,4},{9,5},{1... | collective-permute-start | bytes 589832 | tf_op jit(solution)/shard_map/ppermute | solution.py:231
  8.5 14.1 %collective-permute-start.6 = (f32[48,1024]{1,0:T(8,128)}, f32[48,1024]{1,0:T(8,128)}, u32[]{:S(2)}, u32[]{:S(2)}) collective-permute-start(f32[48,1024]{1,0:T(8,128)} %slice.3.refs_0_), channel_id=1, source_target_pairs={{0,4},{1,5},{2,6},{3,7},{4,8},{5,9},{6,10},{7,11},{8,12},{9,13},{1... | collective-permute-start | bytes 589832 | tf_op jit(solution)/shard_map/ppermute | solution.py:231
  8.5 18.0 %collective-permute-start.4 = (f32[48,1024]{1,0:T(8,128)}, f32[48,1024]{1,0:T(8,128)}, u32[]{:S(2)}, u32[]{:S(2)}) collective-permute-start(f32[48,1024]{1,0:T(8,128)} %slice.3.refs_0_), channel_id=1, source_target_pairs={{0,14},{1,15},{2,0},{3,1},{4,2},{5,3},{6,4},{7,5},{8,6},{9,7},{10,... | collective-permute-start | bytes 589832 | tf_op jit(solution)/shard_map/ppermute | solution.py:231
  11.6 14.9 %collective-permute-start.3 = (f32[48,1024]{1,0:T(8,128)}, f32[48,1024]{1,0:T(8,128)}, u32[]{:S(2)}, u32[]{:S(2)}) collective-permute-start(f32[48,1024]{1,0:T(8,128)} %slice.3.refs_0_), channel_id=1, source_target_pairs={{0,2},{1,3},{2,4},{3,5},{4,6},{5,7},{6,8},{7,9},{8,10},{9,11},{10,... | collective-permute-start | bytes 589832 | tf_op jit(solution)/shard_map/ppermute | solution.py:231
  11.6 1.9 %copy-start.2 = (f32[48,16384]{1,0:T(8,128)S(1)}, f32[48,16384]{1,0:T(8,128)}, u32[]{:S(2)}) copy-start(f32[48,16384]{1,0:T(8,128)} %w_ref.1) | copy-start | bytes 9437188
  15.4 10.1 %collective-permute-start.2 = (f32[32,512]{1,0:T(8,128)S(1)}, f32[32,512]{1,0:T(8,128)S(1)}, u32[]{:S(2)}, u32[]{:S(2)}) collective-permute-start(f32[32,512]{1,0:T(8,128)S(1)} %shard_map.38.own_ref), channel_id=1, source_target_pairs={{1,13},{17,29},{33,45},{49,61},{65,77},{81,93},{97,109},{113,125},... | collective-permute-start | bytes 196616 | tf_op jit(solution)/shard_map/ppermute | solution.py:231
  19.2 7.3 %collective-permute-start.1 = (f32[32,512]{1,0:T(8,128)S(1)}, f32[32,512]{1,0:T(8,128)S(1)}, u32[]{:S(2)}, u32[]{:S(2)}) collective-permute-start(f32[32,512]{1,0:T(8,128)S(1)} %shard_map.38.own_ref), channel_id=1, source_target_pairs={{1,9},{17,25},{33,41},{49,57},{65,73},{81,89},{97,105},{113,121},{... | collective-permute-start | bytes 196616 | tf_op jit(solution)/shard_map/ppermute | solution.py:231
  22.6 3.9 %collective-permute-start = (f32[32,512]{1,0:T(8,128)S(1)}, f32[32,512]{1,0:T(8,128)S(1)}, u32[]{:S(2)}, u32[]{:S(2)}) collective-permute-start(f32[32,512]{1,0:T(8,128)S(1)} %shard_map.38.own_ref), channel_id=1, source_target_pairs={{1,5},{17,21},{33,37},{49,53},{65,69},{81,85},{97,101},{113,117},{... | collective-permute-start | bytes 196616 | tf_op jit(solution)/shard_map/ppermute | solution.py:231
  25.5 10.4 %collective-permute-start.10 = (f32[48,1024]{1,0:T(8,128)}, f32[48,1024]{1,0:T(8,128)}, u32[]{:S(2)}, u32[]{:S(2)}) collective-permute-start(f32[48,1024]{1,0:T(8,128)} %broadcast_select_fusion), channel_id=1, source_target_pairs={{0,4},{1,13},{2,6},{3,15},{4,8},{5,1},{6,10},{7,3},{8,12},{9,5},{1... | collective-permute-start | bytes 589832 | tf_op jit(solution)/shard_map/ppermute | solution.py:231
  26.5 9.4 %collective-permute-start.9 = (f32[48,1024]{1,0:T(8,128)}, f32[48,1024]{1,0:T(8,128)}, u32[]{:S(2)}, u32[]{:S(2)}) collective-permute-start(f32[48,1024]{1,0:T(8,128)} %collective-permute-done.7.refs_4_), channel_id=1, source_target_pairs={{0,14},{1,15},{2,0},{3,1},{4,2},{5,3},{6,4},{7,5},{8,6},{9,7},{10,... | collective-permute-start | bytes 589832 | tf_op jit(solution)/shard_map/ppermute | solution.py:231
  26.6 10.6 %collective-permute-start.8 = (f32[48,1024]{1,0:T(8,128)}, f32[48,1024]{1,0:T(8,128)}, u32[]{:S(2)}, u32[]{:S(2)}) collective-permute-start(f32[48,1024]{1,0:T(8,128)} %collective-permute-done.6.refs_3_), channel_id=1, source_target_pairs={{0,2},{1,3},{2,4},{3,5},{4,6},{5,7},{6,8},{7,9},{8,10},{9,11},{10,... | collective-permute-start | bytes 589832 | tf_op jit(solution)/shard_map/ppermute | solution.py:231
  28.1 9.1 %copy-start.3 = (f32[2,32,512]{2,1,0:T(8,128)S(1)}, f32[2,32,512]{2,1,0:T(8,128)}, u32[]{:S(2)}) copy-start(f32[2,32,512]{2,1,0:T(8,128)} %inverse_ref.1) | copy-start | bytes 393220
  28.1 7.7 %collective-permute-start.5 = (f32[32,512]{1,0:T(8,128)S(1)}, f32[32,512]{1,0:T(8,128)S(1)}, u32[]{:S(2)}, u32[]{:S(2)}) collective-permute-start(f32[32,512]{1,0:T(8,128)S(1)} %shard_map.39.slab_ref), channel_id=1, source_target_pairs={{1,3},{5,7},{9,11},{13,15},{17,19},{21,23},{25,27},{29,31},{33,35}... | collective-permute-start | bytes 196616 | tf_op jit(solution)/shard_map/ppermute | solution.py:231
  30.4 75.5 %all-to-all-start = ((f32[16,8,48,128]{3,2,1,0:T(8,128)}), f32[16,8,48,128]{3,2,1,0:T(8,128)}, u32[]{:S(2)}, u32[]{:S(2)}) async-start(f32[16,8,48,128]{3,2,1,0:T(8,128)} %shard_map.37), calls=%async_computation | async-start | bytes 6291456 | tf_op jit(solution)/shard_map/all_to_all | solution.py:244
  37.3 5.2 %collective-permute-start.13 = (f32[48,512]{1,0:T(8,128)S(1)}, f32[48,512]{1,0:T(8,128)S(1)}, u32[]{:S(2)}, u32[]{:S(2)}) collective-permute-start(f32[48,512]{1,0:T(8,128)S(1)} %shard_map.40), channel_id=1, source_target_pairs={{0,16},{1,65},{2,18},{3,67},{4,20},{5,69},{6,22},{7,71},{8,24},{9,... | collective-permute-start | bytes 294920 | tf_op jit(solution)/shard_map/ppermute | solution.py:235
  38.5 5.9 %collective-permute-start.12 = (f32[48,512]{1,0:T(8,128)S(1)}, f32[48,512]{1,0:T(8,128)S(1)}, u32[]{:S(2)}, u32[]{:S(2)}) collective-permute-start(f32[48,512]{1,0:T(8,128)S(1)} %shard_map.40), channel_id=1, source_target_pairs={{0,32},{1,129},{2,34},{3,131},{4,36},{5,133},{6,38},{7,135},{8,40}... | collective-permute-start | bytes 294920 | tf_op jit(solution)/shard_map/ppermute | solution.py:235
  41.0 3.9 %collective-permute-start.11 = (f32[48,512]{1,0:T(8,128)S(1)}, f32[48,512]{1,0:T(8,128)S(1)}, u32[]{:S(2)}, u32[]{:S(2)}) collective-permute-start(f32[48,512]{1,0:T(8,128)S(1)} %shard_map.40), channel_id=1, source_target_pairs={{0,48},{1,193},{2,50},{3,195},{4,52},{5,197},{6,54},{7,199},{8,56}... | collective-permute-start | bytes 294920 | tf_op jit(solution)/shard_map/ppermute | solution.py:235
  44.9 8.6 %collective-permute-start.15 = (f32[4,48,512]{2,1,0:T(8,128)S(1)}, f32[4,48,512]{2,1,0:T(8,128)S(1)}, u32[]{:S(2)}, u32[]{:S(2)}) collective-permute-start(f32[4,48,512]{2,1,0:T(8,128)S(1)} %get-tuple-element.44), channel_id=1, source_target_pairs={{0,128},{1,33},{2,130},{3,35},{4,132},{5,37},{6,134},{7,39},{8,136... | collective-permute-start | bytes 1179656 | tf_op jit(solution)/shard_map/ppermute | solution.py:235
  47.9 10.2 %collective-permute-start.14 = (f32[4,48,512]{2,1,0:T(8,128)S(1)}, f32[4,48,512]{2,1,0:T(8,128)S(1)}, u32[]{:S(2)}, u32[]{:S(2)}) collective-permute-start(f32[4,48,512]{2,1,0:T(8,128)S(1)} %get-tuple-element.44), channel_id=1, source_target_pairs={{0,192},{1,49},{2,194},{3,51},{4,196},{5,53},{6,198},{7,55},{8,200... | collective-permute-start | bytes 1179656 | tf_op jit(solution)/shard_map/ppermute | solution.py:235
  48.7 9.4 %collective-permute-start.16 = (f32[4,48,512]{2,1,0:T(8,128)S(1)}, f32[4,48,512]{2,1,0:T(8,128)S(1)}, u32[]{:S(2)}, u32[]{:S(2)}) collective-permute-start(f32[4,48,512]{2,1,0:T(8,128)S(1)} %get-tuple-element.44), channel_id=1, source_target_pairs={{0,64},{1,17},{2,66},{3,19},{4,68},{5,21},{6,70},{7,23},{8,72},{9,... | collective-permute-start | bytes 1179656 | tf_op jit(solution)/shard_map/ppermute | solution.py:235
  58.3 7.0 %collective-permute-start.17 = (f32[16,48,512]{2,1,0:T(8,128)S(1)}, f32[16,48,512]{2,1,0:T(8,128)S(1)}, u32[]{:S(2)}, u32[]{:S(2)}) collective-permute-start(f32[16,48,512]{2,1,0:T(8,128)S(1)} %bitcast.11), channel_id=1, source_target_pairs={{0,1},{1,0},{2,3},{3,2},{4,5},{5,4},{6,7},{7,6},{8,9},{9,8},{10,11... | collective-permute-start | bytes 4718600 | tf_op jit(solution)/shard_map/ppermute | solution.py:231
  65.3 9.2 %copy-start.1 = (f32[2,1,512,1024]{3,2,1,0:T(8,128)S(1)}, f32[2,1,512,1024]{3,2,1,0:T(8,128)}, u32[]{:S(2)}) copy-start(f32[2,1,512,1024]{3,2,1,0:T(8,128)} %panel_ref.2) | copy-start | bytes 12582916
  71.0 3.5 %collective-permute-start.18 = (f32[8,48,1024]{2,1,0:T(8,128)S(1)}, f32[8,48,1024]{2,1,0:T(8,128)S(1)}, u32[]{:S(2)}, u32[]{:S(2)}) collective-permute-start(f32[8,48,1024]{2,1,0:T(8,128)S(1)} %shard_map.41.own_ref), channel_id=1, source_target_pairs={{0,1},{1,0},{2,3},{3,2},{4,5},{5,4},{6,7},{7,6},{8,9},{9,8},{10,11... | collective-permute-start | bytes 4718600 | tf_op jit(solution)/shard_map/ppermute | solution.py:231

commit v4 on v3

--- a/solution.py
+++ b/solution.py
@@ -30,13 +30,13 @@
 def pack_body(w_ref, o_ref):
     for c in range(16):
         for k in range(8):
-            o_ref[c, k] = w_ref[:, pl.ds(((k // 4) * 16 + c) * B + (k % 4) * 128, 128)]
+            o_ref[c, pl.ds(k, 48, stride=8), :] = w_ref[:, pl.ds(((k // 4) * 16 + c) * B + (k % 4) * 128, 128)]
 
 
 def pack(weight):
     return pl.pallas_call(
         pack_body,
-        out_shape=jax.ShapeDtypeStruct((16, 8, 48, 128), jnp.float32),
+        out_shape=jax.ShapeDtypeStruct((16, 384, 128), jnp.float32),
         compiler_params=pltpu.CompilerParams(vmem_limit_bytes=8 << 20),
         cost_estimate=COST,
     )(weight)
@@ -142,14 +142,12 @@
             xh_scr[pl.ds(at, 48)] = high
             xl_scr[pl.ds(at, 48)] = low
 
-    def step(j, carry):
-        h, i = j // 2, j % 2
-        lh, ll = split(panel_ref[h, 0, pl.ds(pl.multiple_of(i * 256, 256), 256), :])
+    for j in range(4):
+        lh, ll = split(panel_ref[j // 2, 0, j % 2 * 256 : j % 2 * 256 + 256, :])
         out = dot_half(xh_scr[...], lh) + (dot_half(xl_scr[...], lh) + dot_half(xh_scr[...], ll))
-        p_ref[:, :, pl.ds(pl.multiple_of(j * 256, 256), 256)] = out.reshape(16, 48, 256)
-        return carry
-
-    lax.fori_loop(0, 4, step, 0)
+        for s in range(16):
+            for t in range(2):
+                p_ref[s, pl.ds(2 * j + t, 48, stride=8), :] = out[48 * s : 48 * s + 48, t * 128 : t * 128 + 128]
 
     for which in range(2):
 
@@ -157,13 +155,15 @@
         def _():
             for part, ref in ((parity, own_ref), (1 - parity, other_ref)):
                 for z in range(8):
-                    p_ref[2 * z + part, :, :B] = -ref[z, :, which * B : which * B + B]
+                    for k in range(4):
+                        lanes = slice(which * B + k * 128, which * B + k * 128 + 128)
+                        p_ref[2 * z + part, pl.ds(k, 48, stride=8), :] = -ref[z, :, lanes]
 
 
 def product(own, other, panel):
     return pl.pallas_call(
         product_body,
-        out_shape=jax.ShapeDtypeStruct((16, 48, 2 * B), jnp.float32),
+        out_shape=jax.ShapeDtypeStruct((16, 384, 128), jnp.float32),
         scratch_shapes=[
             pltpu.VMEM((768, 2 * B), jnp.bfloat16),
             pltpu.VMEM((768, 2 * B), jnp.bfloat16),
@@ -174,18 +174,15 @@
 
 
 def finish_body(part_ref, p_ref, o_ref, w_scr, scr, in_sems, out_sems):
-    solved = lax.axis_index("cols") < 2
+    half = lax.broadcasted_iota(jnp.int32, (384, 128), 0) % 8
+    drop = (half < 4) & (lax.axis_index("cols") < 2)
     reads = [pltpu.make_async_copy(part_ref.at[s], w_scr.at[s], in_sems.at[s]) for s in range(16)]
     writes = [pltpu.make_async_copy(scr.at[s], o_ref.at[s], out_sems.at[s]) for s in range(16)]
     for read in reads:
         read.start()
     for s in range(16):
         reads[s].wait()
-        for k in range(8):
-            w = w_scr[s, k]
-            if k < 4:
-                w = jnp.where(solved, jnp.zeros_like(w), w)
-            scr[s, pl.ds(k, 48, stride=8), :] = w - p_ref[s, :, k * 128 : k * 128 + 128]
+        scr[s] = jnp.where(drop, 0.0, w_scr[s]) - p_ref[s]
         writes[s].start()
     for write in writes:
         write.wait()
@@ -198,7 +195,7 @@
         in_specs=[pl.BlockSpec(memory_space=pl.ANY), pl.BlockSpec(memory_space=pltpu.VMEM)],
         out_specs=pl.BlockSpec(memory_space=pl.ANY),
         scratch_shapes=[
-            pltpu.VMEM((16, 8, 48, 128), jnp.float32),
+            pltpu.VMEM((16, 384, 128), jnp.float32),
             pltpu.VMEM((16, 384, 128), jnp.float32),
             pltpu.SemaphoreType.DMA((16,)),
             pltpu.SemaphoreType.DMA((16,)),

time: 110 us -> 110 us (level)
  no operation moved by 1% of the time
where the time goes in v4:
time: 110 us; the launch traced here: 109 us
  waiting for transfers between devices  45.7 us (42%)
  starting transfers between devices  41 us (37%)
  Pallas kernels  16.8 us (15%)
  local copies, waits for them, and re-layouts  3.51 us (3%)
  other arithmetic  1.88 us (2%)
    ppermute x13, starting transfers between devices, along(): return lax.ppermute(value, 'cols', pairs)  27.2 us
    all_to_all x1, waiting for transfers between devices, exchange(): return lax.all_to_all(part, 'cols', split_axis=0, concat_axis=0, tiled=True)  25.8 us
    ppermute x6, waiting for transfers between devices, plane_step(): lax.ppermute(value, ('rows', 'cols'), plane_shift(a, phase))  11.5 us
    ppermute x6, starting transfers between devices, plane_step(): lax.ppermute(value, ('rows', 'cols'), plane_shift(a, phase))  9.36 us
    ppermute x13, waiting for transfers between devices, along(): return lax.ppermute(value, 'cols', pairs)  8.43 us
    pallas_call x1, Pallas kernels, solve(): pl.pallas_call(solve_body, out_shape=jax.ShapeDtypeStruct((8, 48, 2 * B),...  5.67 us
    pallas_call x1, Pallas kernels, product(): pl.pallas_call(product_body, out_shape=jax.ShapeDtypeStruct((16, 384, 128...  5.63 us
    all_to_all x1, starting transfers between devices, exchange(): return lax.all_to_all(part, 'cols', split_axis=0, concat_axis=0, tiled=True)  4.45 us
  transfers between devices with their start and end apart: 20, of which 11 were waited for; matrix products, arithmetic and copies ran while one was open for 2% of the time, Pallas kernels for 13%

profile of v4, /device:TPU:1, one launch (start us, length us, event | category | flops | bytes accessed | tf_op | source)
XLA Modules:
  0.0 109.3 jit_solution(3163817311764567884)
XLA Ops:
  0.0 1.6 %slice.3.refs_0_ = f32[48,1024]{1,0:T(8,128)} slice(f32[48,16384]{1,0:T(8,128)} %w_ref.1), slice={[0:48], [0:1024]} | slice | bytes 393216 | tf_op jit(solution)/shard_map/slice | solution.py:245
  1.6 6.8 %collective-permute-start.7 = (f32[48,1024]{1,0:T(8,128)}, f32[48,1024]{1,0:T(8,128)}, u32[]{:S(2)}, u32[]{:S(2)}) collective-permute-start(f32[48,1024]{1,0:T(8,128)} %slice.3.refs_0_), channel_id=1, source_target_pairs={{0,12},{1,13},{2,14},{3,15},{4,0},{5,1},{6,2},{7,3},{8,4},{9,5},{1... | collective-permute-start | bytes 589832 | tf_op jit(solution)/shard_map/ppermute | solution.py:228
  8.5 0.0 collective-permute-start.6
  8.5 3.1 %collective-permute-start.4 = (f32[48,1024]{1,0:T(8,128)}, f32[48,1024]{1,0:T(8,128)}, u32[]{:S(2)}, u32[]{:S(2)}) collective-permute-start(f32[48,1024]{1,0:T(8,128)} %slice.3.refs_0_), channel_id=1, source_target_pairs={{0,14},{1,15},{2,0},{3,1},{4,2},{5,3},{6,4},{7,5},{8,6},{9,7},{10,... | collective-permute-start | bytes 589832 | tf_op jit(solution)/shard_map/ppermute | solution.py:228
  11.6 0.0 collective-permute-start.3
  11.6 1.9 %copy-done.2 = f32[48,16384]{1,0:T(8,128)S(1)} copy-done((f32[48,16384]{1,0:T(8,128)S(1)}, f32[48,16384]{1,0:T(8,128)}, u32[]{:S(2)}) %copy-start.2) | copy-done | bytes 3145752
  13.5 2.3 %shard_map.37 = f32[16,384,128]{2,1,0:T(8,128)} custom-call(f32[48,16384]{1,0:T(8,128)S(1)} %copy-done.2), custom_call_target="tpu_custom_call" | custom-call | flops 1024 | bytes 1024 | tf_op jit(solution)/shard_map/pallas_call | solution.py:37
  15.8 3.8 %collective-permute-start.2 = (f32[32,512]{1,0:T(8,128)S(1)}, f32[32,512]{1,0:T(8,128)S(1)}, u32[]{:S(2)}, u32[]{:S(2)}) collective-permute-start(f32[32,512]{1,0:T(8,128)S(1)} %shard_map.38.own_ref), channel_id=1, source_target_pairs={{1,13},{17,29},{33,45},{49,61},{65,77},{81,93},{97,109},{113,125},... | collective-permute-start | bytes 196616 | tf_op jit(solution)/shard_map/ppermute | solution.py:228
  19.7 0.0 collective-permute-done.7.refs_4_
  19.7 2.9 %collective-permute-start.1 = (f32[32,512]{1,0:T(8,128)S(1)}, f32[32,512]{1,0:T(8,128)S(1)}, u32[]{:S(2)}, u32[]{:S(2)}) collective-permute-start(f32[32,512]{1,0:T(8,128)S(1)} %shard_map.38.own_ref), channel_id=1, source_target_pairs={{1,9},{17,25},{33,41},{49,57},{65,73},{81,89},{97,105},{113,121},{... | collective-permute-start | bytes 196616 | tf_op jit(solution)/shard_map/ppermute | solution.py:228
  22.6 0.0 collective-permute-done.6.refs_3_
  22.6 1.3 %collective-permute-start = (f32[32,512]{1,0:T(8,128)S(1)}, f32[32,512]{1,0:T(8,128)S(1)}, u32[]{:S(2)}, u32[]{:S(2)}) collective-permute-start(f32[32,512]{1,0:T(8,128)S(1)} %shard_map.38.own_ref), channel_id=1, source_target_pairs={{1,5},{17,21},{33,37},{49,53},{65,69},{81,85},{97,101},{113,117},{... | collective-permute-start | bytes 196616 | tf_op jit(solution)/shard_map/ppermute | solution.py:228
  23.9 1.7 %broadcast_select_fusion = f32[48,1024]{1,0:T(8,128)} fusion(f32[48,1024]{1,0:T(8,128)} %collective-permute-done.6.refs_3_, f32[48,1024]{1,0:T(8,128)} %collective-permute-done.7.refs_4_, pred[]{:T(512)S(6)} %eq.5), kind=kLoop, calls=%fused_computation.2 | loop fusion | flops 49152 | bytes 589825 | tf_op jit(solution)/shard_map/jit(_where)/select_n | solution.py:254
  25.5 0.0 collective-permute-done.2.refs_2_
  25.5 1.0 collective-permute-start.10
  26.5 0.0 collective-permute-done.1.refs_1_
  26.5 0.0 collective-permute-done.3.refs_1_
  26.5 0.1 collective-permute-start.9
  26.6 1.5 %collective-permute-start.8 = (f32[48,1024]{1,0:T(8,128)}, f32[48,1024]{1,0:T(8,128)}, u32[]{:S(2)}, u32[]{:S(2)}) collective-permute-start(f32[48,1024]{1,0:T(8,128)} %collective-permute-done.6.refs_3_), channel_id=1, source_target_pairs={{0,2},{1,3},{2,4},{3,5},{4,6},{5,7},{6,8},{7,9},{8,10},{9,11},{10,... | collective-permute-start | bytes 589832 | tf_op jit(solution)/shard_map/ppermute | solution.py:228
  28.1 0.0 copy-start.3
  28.1 2.3 %collective-permute-start.5 = (f32[32,512]{1,0:T(8,128)S(1)}, f32[32,512]{1,0:T(8,128)S(1)}, u32[]{:S(2)}, u32[]{:S(2)}) collective-permute-start(f32[32,512]{1,0:T(8,128)S(1)} %shard_map.39.slab_ref), channel_id=1, source_target_pairs={{1,3},{5,7},{9,11},{13,15},{17,19},{21,23},{25,27},{29,31},{33,35}... | collective-permute-start | bytes 196616 | tf_op jit(solution)/shard_map/ppermute | solution.py:228
  30.4 4.4 %all-to-all-start = ((f32[16,384,128]{2,1,0:T(8,128)}), f32[16,384,128]{2,1,0:T(8,128)}, u32[]{:S(2)}, u32[]{:S(2)}) async-start(f32[16,384,128]{2,1,0:T(8,128)} %shard_map.37), calls=%async_computation | async-start | bytes 6291456 | tf_op jit(solution)/shard_map/all_to_all | solution.py:241
  34.9 0.9 collective-permute-done.5.got_ref
  35.8 0.1 collective-permute-done.9.refs_6_
  35.9 0.0 collective-permute-done.10.refs_7_
  35.9 1.3 %collective-permute-done.8.refs_5_ = f32[48,1024]{1,0:T(8,128)} collective-permute-done((f32[48,1024]{1,0:T(8,128)}, f32[48,1024]{1,0:T(8,128)}, u32[]{:S(2)}, u32[]{:S(2)}) %collective-permute-start.8) | collective-permute-done | bytes 196640 | tf_op jit(solution)/shard_map/ppermute | solution.py:228
  37.3 1.3 %collective-permute-start.13 = (f32[48,512]{1,0:T(8,128)S(1)}, f32[48,512]{1,0:T(8,128)S(1)}, u32[]{:S(2)}, u32[]{:S(2)}) collective-permute-start(f32[48,512]{1,0:T(8,128)S(1)} %shard_map.40), channel_id=1, source_target_pairs={{0,16},{1,65},{2,18},{3,67},{4,20},{5,69},{6,22},{7,71},{8,24},{9,... | collective-permute-start | bytes 294920 | tf_op jit(solution)/shard_map/ppermute | solution.py:232
  38.5 2.5 %collective-permute-start.12 = (f32[48,512]{1,0:T(8,128)S(1)}, f32[48,512]{1,0:T(8,128)S(1)}, u32[]{:S(2)}, u32[]{:S(2)}) collective-permute-start(f32[48,512]{1,0:T(8,128)S(1)} %shard_map.40), channel_id=1, source_target_pairs={{0,32},{1,129},{2,34},{3,131},{4,36},{5,133},{6,38},{7,135},{8,40}... | collective-permute-start | bytes 294920 | tf_op jit(solution)/shard_map/ppermute | solution.py:232
  41.0 1.2 %collective-permute-start.11 = (f32[48,512]{1,0:T(8,128)S(1)}, f32[48,512]{1,0:T(8,128)S(1)}, u32[]{:S(2)}, u32[]{:S(2)}) collective-permute-start(f32[48,512]{1,0:T(8,128)S(1)} %shard_map.40), channel_id=1, source_target_pairs={{0,48},{1,193},{2,50},{3,195},{4,52},{5,197},{6,54},{7,199},{8,56}... | collective-permute-start | bytes 294920 | tf_op jit(solution)/shard_map/ppermute | solution.py:232
  42.2 0.3 collective-permute-done.13
  42.4 2.0 %collective-permute-done.12 = f32[48,512]{1,0:T(8,128)S(1)} collective-permute-done((f32[48,512]{1,0:T(8,128)S(1)}, f32[48,512]{1,0:T(8,128)S(1)}, u32[]{:S(2)}, u32[]{:S(2)}) %collective-permute-start.12) | collective-permute-done | bytes 98336 | tf_op jit(solution)/shard_map/ppermute | solution.py:232
  44.5 0.4 collective-permute-done.11
  44.9 0.1 fusion
  44.9 3.0 %collective-permute-start.15 = (f32[4,48,512]{2,1,0:T(8,128)S(1)}, f32[4,48,512]{2,1,0:T(8,128)S(1)}, u32[]{:S(2)}, u32[]{:S(2)}) collective-permute-start(f32[4,48,512]{2,1,0:T(8,128)S(1)} %get-tuple-element.44), channel_id=1, source_target_pairs={{0,128},{1,33},{2,130},{3,35},{4,132},{5,37},{6,134},{7,39},{8,136... | collective-permute-start | bytes 1179656 | tf_op jit(solution)/shard_map/ppermute | solution.py:232
  47.9 0.8 collective-permute-start.14
  48.7 0.7 collective-permute-start.16
  49.4 4.2 %collective-permute-done.15 = f32[4,48,512]{2,1,0:T(8,128)S(1)} collective-permute-done((f32[4,48,512]{2,1,0:T(8,128)S(1)}, f32[4,48,512]{2,1,0:T(8,128)S(1)}, u32[]{:S(2)}, u32[]{:S(2)}) %collective-permute-start.15) | collective-permute-done | bytes 393248 | tf_op jit(solution)/shard_map/ppermute | solution.py:232
  53.5 4.6 %collective-permute-done.14 = f32[4,48,512]{2,1,0:T(8,128)S(1)} collective-permute-done((f32[4,48,512]{2,1,0:T(8,128)S(1)}, f32[4,48,512]{2,1,0:T(8,128)S(1)}, u32[]{:S(2)}, u32[]{:S(2)}) %collective-permute-start.14) | collective-permute-done | bytes 393248 | tf_op jit(solution)/shard_map/ppermute | solution.py:232
  58.1 0.0 collective-permute-done.16
  58.1 0.2 pad_maximum_fusion
  58.3 4.0 %collective-permute-start.17 = (f32[16,48,512]{2,1,0:T(8,128)S(1)}, f32[16,48,512]{2,1,0:T(8,128)S(1)}, u32[]{:S(2)}, u32[]{:S(2)}) collective-permute-start(f32[16,48,512]{2,1,0:T(8,128)S(1)} %bitcast.11), channel_id=1, source_target_pairs={{0,1},{1,0},{2,3},{3,2},{4,5},{5,4},{6,7},{7,6},{8,9},{9,8},{10,11... | collective-permute-start | bytes 4718600 | tf_op jit(solution)/shard_map/ppermute | solution.py:228
  62.3 3.0 %collective-permute-done.17.other_ref = f32[16,48,512]{2,1,0:T(8,128)S(1)} collective-permute-done((f32[16,48,512]{2,1,0:T(8,128)S(1)}, f32[16,48,512]{2,1,0:T(8,128)S(1)}, u32[]{:S(2)}, u32[]{:S(2)}) %collective-permute-start.17) | collective-permute-done | bytes 1572896 | tf_op jit(solution)/shard_map/ppermute | solution.py:228
  65.3 5.7 %shard_map.41.own_ref = f32[8,48,1024]{2,1,0:T(8,128)S(1)} custom-call(f32[16,48,512]{2,1,0:T(8,128)S(1)} %bitcast.12, f32[16,48,512]{2,1,0:T(8,128)S(1)} %collective-permute-done.17.other_ref, f32[48,1024]{1,0:T(8,128)} %slice.3.refs_0_, f32[48,1024]{1,0:T(8,128)} %collective-permute-done.3.refs_1_, f32[48,1024]{1,0:T(8,128)} %collective-permute-done.4.refs_2_, ...), custom_call_target="tpu_custom_call" | custom-call | flops 1024 | bytes 1024 | tf_op jit(solution)/shard_map/pallas_call | solution.py:120
  71.0 0.5 collective-permute-start.18
  71.5 3.0 %collective-permute-done.18.other_ref = f32[8,48,1024]{2,1,0:T(8,128)S(1)} collective-permute-done((f32[8,48,1024]{2,1,0:T(8,128)S(1)}, f32[8,48,1024]{2,1,0:T(8,128)S(1)}, u32[]{:S(2)}, u32[]{:S(2)}) %collective-permute-start.18) | collective-permute-done | bytes 1572896 | tf_op jit(solution)/shard_map/ppermute | solution.py:228
  74.5 5.6 %shard_map.42.p_ref = f32[16,384,128]{2,1,0:T(8,128)S(1)} custom-call(f32[8,48,1024]{2,1,0:T(8,128)S(1)} %shard_map.41.own_ref, f32[8,48,1024]{2,1,0:T(8,128)S(1)} %collective-permute-done.18.other_ref, f32[2,1,512,1024]{3,2,1,0:T(8,128)S(1)} %copy-done.1), custom_call_target="tpu_custom_call" | custom-call | flops 1024 | bytes 1024 | tf_op jit(solution)/shard_map/pallas_call | solution.py:164
  80.1 25.8 %all-to-all-done.part_ref = f32[16,384,128]{2,1,0:T(8,128)} async-done(((f32[16,384,128]{2,1,0:T(8,128)}), f32[16,384,128]{2,1,0:T(8,128)}, u32[]{:S(2)}, u32[]{:S(2)}) %all-to-all-start) | async-done | bytes 3145760 | tf_op jit(solution)/shard_map/all_to_all | solution.py:241
  106.0 3.1 %shard_map.43 = f32[16,384,128]{2,1,0:T(8,128)} custom-call(f32[16,384,128]{2,1,0:T(8,128)} %all-to-all-done.part_ref, f32[16,384,128]{2,1,0:T(8,128)S(1)} %shard_map.42.p_ref), custom_call_target="tpu_custom_call" | custom-call | flops 1024 | bytes 1024 | tf_op jit(solution)/shard_map/pallas_call | solution.py:192
  (11 shorter events, 0.1 us)
Async XLA Ops:
  1.6 14.2 %copy-start = (f32[2,1,512,1024]{3,2,1,0:T(8,128)S(1)}, f32[2,1,512,1024]{3,2,1,0:T(8,128)}, u32[]{:S(2)}) copy-start(f32[2,1,512,1024]{3,2,1,0:T(8,128)} %panel_ref.2) | copy-start | bytes 12582916
  1.6 18.0 %collective-permute-start.7 = (f32[48,1024]{1,0:T(8,128)}, f32[48,1024]{1,0:T(8,128)}, u32[]{:S(2)}, u32[]{:S(2)}) collective-permute-start(f32[48,1024]{1,0:T(8,128)} %slice.3.refs_0_), channel_id=1, source_target_pairs={{0,12},{1,13},{2,14},{3,15},{4,0},{5,1},{6,2},{7,3},{8,4},{9,5},{1... | collective-permute-start | bytes 589832 | tf_op jit(solution)/shard_map/ppermute | solution.py:228
  8.5 14.1 %collective-permute-start.6 = (f32[48,1024]{1,0:T(8,128)}, f32[48,1024]{1,0:T(8,128)}, u32[]{:S(2)}, u32[]{:S(2)}) collective-permute-start(f32[48,1024]{1,0:T(8,128)} %slice.3.refs_0_), channel_id=1, source_target_pairs={{0,4},{1,5},{2,6},{3,7},{4,8},{5,9},{6,10},{7,11},{8,12},{9,13},{1... | collective-permute-start | bytes 589832 | tf_op jit(solution)/shard_map/ppermute | solution.py:228
  8.5 18.0 %collective-permute-start.4 = (f32[48,1024]{1,0:T(8,128)}, f32[48,1024]{1,0:T(8,128)}, u32[]{:S(2)}, u32[]{:S(2)}) collective-permute-start(f32[48,1024]{1,0:T(8,128)} %slice.3.refs_0_), channel_id=1, source_target_pairs={{0,14},{1,15},{2,0},{3,1},{4,2},{5,3},{6,4},{7,5},{8,6},{9,7},{10,... | collective-permute-start | bytes 589832 | tf_op jit(solution)/shard_map/ppermute | solution.py:228
  11.6 14.9 %collective-permute-start.3 = (f32[48,1024]{1,0:T(8,128)}, f32[48,1024]{1,0:T(8,128)}, u32[]{:S(2)}, u32[]{:S(2)}) collective-permute-start(f32[48,1024]{1,0:T(8,128)} %slice.3.refs_0_), channel_id=1, source_target_pairs={{0,2},{1,3},{2,4},{3,5},{4,6},{5,7},{6,8},{7,9},{8,10},{9,11},{10,... | collective-permute-start | bytes 589832 | tf_op jit(solution)/shard_map/ppermute | solution.py:228
  11.6 1.9 %copy-start.2 = (f32[48,16384]{1,0:T(8,128)S(1)}, f32[48,16384]{1,0:T(8,128)}, u32[]{:S(2)}) copy-start(f32[48,16384]{1,0:T(8,128)} %w_ref.1) | copy-start | bytes 9437188
  15.8 9.7 %collective-permute-start.2 = (f32[32,512]{1,0:T(8,128)S(1)}, f32[32,512]{1,0:T(8,128)S(1)}, u32[]{:S(2)}, u32[]{:S(2)}) collective-permute-start(f32[32,512]{1,0:T(8,128)S(1)} %shard_map.38.own_ref), channel_id=1, source_target_pairs={{1,13},{17,29},{33,45},{49,61},{65,77},{81,93},{97,109},{113,125},... | collective-permute-start | bytes 196616 | tf_op jit(solution)/shard_map/ppermute | solution.py:228
  19.7 6.8 %collective-permute-start.1 = (f32[32,512]{1,0:T(8,128)S(1)}, f32[32,512]{1,0:T(8,128)S(1)}, u32[]{:S(2)}, u32[]{:S(2)}) collective-permute-start(f32[32,512]{1,0:T(8,128)S(1)} %shard_map.38.own_ref), channel_id=1, source_target_pairs={{1,9},{17,25},{33,41},{49,57},{65,73},{81,89},{97,105},{113,121},{... | collective-permute-start | bytes 196616 | tf_op jit(solution)/shard_map/ppermute | solution.py:228
  22.6 3.9 %collective-permute-start = (f32[32,512]{1,0:T(8,128)S(1)}, f32[32,512]{1,0:T(8,128)S(1)}, u32[]{:S(2)}, u32[]{:S(2)}) collective-permute-start(f32[32,512]{1,0:T(8,128)S(1)} %shard_map.38.own_ref), channel_id=1, source_target_pairs={{1,5},{17,21},{33,37},{49,53},{65,69},{81,85},{97,101},{113,117},{... | collective-permute-start | bytes 196616 | tf_op jit(solution)/shard_map/ppermute | solution.py:228
  25.5 10.4 %collective-permute-start.10 = (f32[48,1024]{1,0:T(8,128)}, f32[48,1024]{1,0:T(8,128)}, u32[]{:S(2)}, u32[]{:S(2)}) collective-permute-start(f32[48,1024]{1,0:T(8,128)} %broadcast_select_fusion), channel_id=1, source_target_pairs={{0,4},{1,13},{2,6},{3,15},{4,8},{5,1},{6,10},{7,3},{8,12},{9,5},{1... | collective-permute-start | bytes 589832 | tf_op jit(solution)/shard_map/ppermute | solution.py:228
  26.5 9.4 %collective-permute-start.9 = (f32[48,1024]{1,0:T(8,128)}, f32[48,1024]{1,0:T(8,128)}, u32[]{:S(2)}, u32[]{:S(2)}) collective-permute-start(f32[48,1024]{1,0:T(8,128)} %collective-permute-done.7.refs_4_), channel_id=1, source_target_pairs={{0,14},{1,15},{2,0},{3,1},{4,2},{5,3},{6,4},{7,5},{8,6},{9,7},{10,... | collective-permute-start | bytes 589832 | tf_op jit(solution)/shard_map/ppermute | solution.py:228
  26.6 10.6 %collective-permute-start.8 = (f32[48,1024]{1,0:T(8,128)}, f32[48,1024]{1,0:T(8,128)}, u32[]{:S(2)}, u32[]{:S(2)}) collective-permute-start(f32[48,1024]{1,0:T(8,128)} %collective-permute-done.6.refs_3_), channel_id=1, source_target_pairs={{0,2},{1,3},{2,4},{3,5},{4,6},{5,7},{6,8},{7,9},{8,10},{9,11},{10,... | collective-permute-start | bytes 589832 | tf_op jit(solution)/shard_map/ppermute | solution.py:228
  28.1 9.1 %copy-start.3 = (f32[2,32,512]{2,1,0:T(8,128)S(1)}, f32[2,32,512]{2,1,0:T(8,128)}, u32[]{:S(2)}) copy-start(f32[2,32,512]{2,1,0:T(8,128)} %inverse_ref.1) | copy-start | bytes 393220
  28.1 7.7 %collective-permute-start.5 = (f32[32,512]{1,0:T(8,128)S(1)}, f32[32,512]{1,0:T(8,128)S(1)}, u32[]{:S(2)}, u32[]{:S(2)}) collective-permute-start(f32[32,512]{1,0:T(8,128)S(1)} %shard_map.39.slab_ref), channel_id=1, source_target_pairs={{1,3},{5,7},{9,11},{13,15},{17,19},{21,23},{25,27},{29,31},{33,35}... | collective-permute-start | bytes 196616 | tf_op jit(solution)/shard_map/ppermute | solution.py:228
  30.4 75.5 %all-to-all-start = ((f32[16,384,128]{2,1,0:T(8,128)}), f32[16,384,128]{2,1,0:T(8,128)}, u32[]{:S(2)}, u32[]{:S(2)}) async-start(f32[16,384,128]{2,1,0:T(8,128)} %shard_map.37), calls=%async_computation | async-start | bytes 6291456 | tf_op jit(solution)/shard_map/all_to_all | solution.py:241
  37.3 5.2 %collective-permute-start.13 = (f32[48,512]{1,0:T(8,128)S(1)}, f32[48,512]{1,0:T(8,128)S(1)}, u32[]{:S(2)}, u32[]{:S(2)}) collective-permute-start(f32[48,512]{1,0:T(8,128)S(1)} %shard_map.40), channel_id=1, source_target_pairs={{0,16},{1,65},{2,18},{3,67},{4,20},{5,69},{6,22},{7,71},{8,24},{9,... | collective-permute-start | bytes 294920 | tf_op jit(solution)/shard_map/ppermute | solution.py:232
  38.5 5.9 %collective-permute-start.12 = (f32[48,512]{1,0:T(8,128)S(1)}, f32[48,512]{1,0:T(8,128)S(1)}, u32[]{:S(2)}, u32[]{:S(2)}) collective-permute-start(f32[48,512]{1,0:T(8,128)S(1)} %shard_map.40), channel_id=1, source_target_pairs={{0,32},{1,129},{2,34},{3,131},{4,36},{5,133},{6,38},{7,135},{8,40}... | collective-permute-start | bytes 294920 | tf_op jit(solution)/shard_map/ppermute | solution.py:232
  41.0 3.9 %collective-permute-start.11 = (f32[48,512]{1,0:T(8,128)S(1)}, f32[48,512]{1,0:T(8,128)S(1)}, u32[]{:S(2)}, u32[]{:S(2)}) collective-permute-start(f32[48,512]{1,0:T(8,128)S(1)} %shard_map.40), channel_id=1, source_target_pairs={{0,48},{1,193},{2,50},{3,195},{4,52},{5,197},{6,54},{7,199},{8,56}... | collective-permute-start | bytes 294920 | tf_op jit(solution)/shard_map/ppermute | solution.py:232
  44.9 8.6 %collective-permute-start.15 = (f32[4,48,512]{2,1,0:T(8,128)S(1)}, f32[4,48,512]{2,1,0:T(8,128)S(1)}, u32[]{:S(2)}, u32[]{:S(2)}) collective-permute-start(f32[4,48,512]{2,1,0:T(8,128)S(1)} %get-tuple-element.44), channel_id=1, source_target_pairs={{0,128},{1,33},{2,130},{3,35},{4,132},{5,37},{6,134},{7,39},{8,136... | collective-permute-start | bytes 1179656 | tf_op jit(solution)/shard_map/ppermute | solution.py:232
  47.9 10.2 %collective-permute-start.14 = (f32[4,48,512]{2,1,0:T(8,128)S(1)}, f32[4,48,512]{2,1,0:T(8,128)S(1)}, u32[]{:S(2)}, u32[]{:S(2)}) collective-permute-start(f32[4,48,512]{2,1,0:T(8,128)S(1)} %get-tuple-element.44), channel_id=1, source_target_pairs={{0,192},{1,49},{2,194},{3,51},{4,196},{5,53},{6,198},{7,55},{8,200... | collective-permute-start | bytes 1179656 | tf_op jit(solution)/shard_map/ppermute | solution.py:232
  48.7 9.4 %collective-permute-start.16 = (f32[4,48,512]{2,1,0:T(8,128)S(1)}, f32[4,48,512]{2,1,0:T(8,128)S(1)}, u32[]{:S(2)}, u32[]{:S(2)}) collective-permute-start(f32[4,48,512]{2,1,0:T(8,128)S(1)} %get-tuple-element.44), channel_id=1, source_target_pairs={{0,64},{1,17},{2,66},{3,19},{4,68},{5,21},{6,70},{7,23},{8,72},{9,... | collective-permute-start | bytes 1179656 | tf_op jit(solution)/shard_map/ppermute | solution.py:232
  58.3 7.0 %collective-permute-start.17 = (f32[16,48,512]{2,1,0:T(8,128)S(1)}, f32[16,48,512]{2,1,0:T(8,128)S(1)}, u32[]{:S(2)}, u32[]{:S(2)}) collective-permute-start(f32[16,48,512]{2,1,0:T(8,128)S(1)} %bitcast.11), channel_id=1, source_target_pairs={{0,1},{1,0},{2,3},{3,2},{4,5},{5,4},{6,7},{7,6},{8,9},{9,8},{10,11... | collective-permute-start | bytes 4718600 | tf_op jit(solution)/shard_map/ppermute | solution.py:228
  65.3 9.2 %copy-start.1 = (f32[2,1,512,1024]{3,2,1,0:T(8,128)S(1)}, f32[2,1,512,1024]{3,2,1,0:T(8,128)}, u32[]{:S(2)}) copy-start(f32[2,1,512,1024]{3,2,1,0:T(8,128)} %panel_ref.2) | copy-start | bytes 12582916
  71.0 3.5 %collective-permute-start.18 = (f32[8,48,1024]{2,1,0:T(8,128)S(1)}, f32[8,48,1024]{2,1,0:T(8,128)S(1)}, u32[]{:S(2)}, u32[]{:S(2)}) collective-permute-start(f32[8,48,1024]{2,1,0:T(8,128)S(1)} %shard_map.41.own_ref), channel_id=1, source_target_pairs={{0,1},{1,0},{2,3},{3,2},{4,5},{5,4},{6,7},{7,6},{8,9},{9,8},{10,11... | collective-permute-start | bytes 4718600 | tf_op jit(solution)/shard_map/ppermute | solution.py:228
